TPU v7x, 32 devices: a whole 2x2x4 slice. The times are simulated.
32 devices in a mesh: wide: 8 (over z, y), narrow: 4 (over x, core).
Axes of the slice: x: 2, y: 2, z: 4, core: 2. Of those that a mesh axis runs over, the one named last changes fastest.
Arguments:
- resid: bfloat16 [32768, 767], P(('wide', 'narrow')), may hold values from -6 to 6
- gain_attn: bfloat16 [768], P(('wide', 'narrow')), may hold values from 0.25 to 1.75
- qkv_weight: bfloat16 [768, 2304], P(('wide', 'narrow')), may hold values from -0.21875 to 0.21875
- qv_bias: bfloat16 [1536], P(('wide', 'narrow')), may hold values from -1.796875 to 1.796875
- out_weight: bfloat16 [768, 767], P(('wide', 'narrow')), may hold values from -1.75 to 1.75
- out_bias: bfloat16 [767], replicated, may hold values from -1.796875 to 1.796875
- gain_mlp: bfloat16 [768], P(('wide', 'narrow')), may hold values from 0.25 to 1.75
- up_weight: bfloat16 [768, 3072], P(('wide', 'narrow')), may hold values from -0.21875 to 0.21875
- up_bias: bfloat16 [3072], P(('wide', 'narrow')), may hold values from -1.796875 to 1.796875
- down_weight: bfloat16 [3072, 767], P(('wide', 'narrow')), may hold values from -0.15625 to 0.15625
- down_bias: bfloat16 [767], replicated, may hold values from -1.796875 to 1.796875
- cotangent: bfloat16 [32768, 767], P(('wide', 'narrow')), may hold values from -6 to 6
- seq_lengths: int32 [32, 4], P(('wide', 'narrow')), may hold values from 0 to 1024, as said below
Outputs:
- out_resid: bfloat16 [32768, 767], P(('wide', 'narrow'))
- grad_resid: bfloat16 [32768, 767], P(('wide', 'narrow'))
- grad_gain_attn: float32 [768], P(('wide', 'narrow'))
- grad_qkv_weight: float32 [768, 2304], P(('wide', 'narrow'))
- grad_qv_bias: float32 [1536], P(('wide', 'narrow'))
- grad_out_weight: float32 [768, 767], P(('wide', 'narrow'))
- grad_out_bias: float32 [767], replicated
- grad_gain_mlp: float32 [768], P(('wide', 'narrow'))
- grad_up_weight: float32 [768, 3072], P(('wide', 'narrow'))
- grad_up_bias: float32 [3072], P(('wide', 'narrow'))
- grad_down_weight: float32 [3072, 767], P(('wide', 'narrow'))
- grad_down_bias: float32 [767], replicated
Inputs may be any that keep to these rules, and one draw needn't show every extreme that they name: `seq_lengths`: each row holds the lengths of one device's sequences, each 512 or 1024, followed by zeros; a row sums to 1024.
All inputs are finite; a program needn't handle non-finite values.
Results may differ from a plain program's by a relative error of at most 0.013.
Values may be sent and summed in bfloat16 or wider, within the bound.
A program may use at most 256 MiB of HBM per device.

v0:
```python
from functools import partial

import jax
import jax.numpy as jnp
from jax import lax
from jax.sharding import PartitionSpec as P

D = 768
H = 12
HD = 64


norm_eps = 1e-05
masked_score = -1e30


def compressed_norm(values, gain_vec):
    row_total = jnp.sum(values, axis=-1, keepdims=True)
    full_vector = jnp.concatenate([values, -row_total], axis=-1)
    mean_sq = jnp.mean(full_vector * full_vector, axis=-1, keepdims=True)
    return full_vector * lax.rsqrt(mean_sq + norm_eps) * gain_vec


def contract_rows(left_side, right_side):
    return lax.dot_general(
        left_side, right_side, (((0,), (0,)), ((), ())), preferred_element_type=jnp.float32
    )


def contract_cols(left_side, right_side):
    return lax.dot_general(
        left_side, right_side, (((1,), (1,)), ((), ())), preferred_element_type=jnp.float32
    )


def segment_ids(lengths, row_count):
    places = jnp.arange(row_count, dtype=jnp.int32)
    seq_ends = jnp.cumsum(lengths)
    segment = jnp.sum((places[:, None] >= seq_ends[None, :]).astype(jnp.int32), axis=1)
    return (places, segment)


def block_scores(query_block, key_heads, places, segment, first_row, last_row):
    scores = jnp.einsum(
        "qhd,khd->hqk", query_block, key_heads[:last_row], preferred_element_type=jnp.float32
    ) * HD ** (-0.5)
    allowed = (segment[first_row:last_row, None] == segment[None, :last_row]) & (
        places[None, :last_row] <= places[first_row:last_row, None]
    )
    return jnp.where(allowed[None], scores, masked_score)


def attend_forward(query_heads, key_heads, value_heads, places, segment):
    row_count = query_heads.shape[0]
    block_rows = min(512, row_count)
    mixed_parts = []
    log_parts = []
    for block_index in range(row_count // block_rows):
        first_row = block_index * block_rows
        last_row = first_row + block_rows
        scores = block_scores(
            query_heads[first_row:last_row], key_heads, places, segment, first_row, last_row
        )
        row_max = jnp.max(scores, axis=-1, keepdims=True)
        exp_scores = jnp.exp(scores - row_max)
        summed = jnp.sum(exp_scores, axis=-1, keepdims=True)
        attn_probs = (exp_scores / summed).astype(jnp.bfloat16)
        mixed_parts.append(
            jnp.einsum(
                "hqk,khd->qhd",
                attn_probs,
                value_heads[:last_row],
                preferred_element_type=jnp.float32,
            )
        )
        log_parts.append(row_max + jnp.log(summed))
    return (jnp.concatenate(mixed_parts, axis=0), jnp.concatenate(log_parts, axis=1))


def attend_backward(query_heads, key_heads, value_heads, grad_mixed, log_sums, places, segment):
    row_count = query_heads.shape[0]
    block_rows = min(512, row_count)
    grad_query_parts = []
    grad_keys = jnp.zeros(key_heads.shape, jnp.float32)
    grad_values = jnp.zeros(value_heads.shape, jnp.float32)
    for block_index in range(row_count // block_rows):
        first_row = block_index * block_rows
        last_row = first_row + block_rows
        query_block = query_heads[first_row:last_row]
        grad_block = grad_mixed[first_row:last_row]
        scores = block_scores(query_block, key_heads, places, segment, first_row, last_row)
        attn_probs = jnp.exp(scores - log_sums[:, first_row:last_row])
        grad_probs = jnp.einsum(
            "qhd,khd->hqk", grad_block, value_heads[:last_row], preferred_element_type=jnp.float32
        )
        row_dot = jnp.sum(attn_probs * grad_probs, axis=-1, keepdims=True)
        grad_scores = (attn_probs * (grad_probs - row_dot)).astype(jnp.bfloat16)
        grad_query_parts.append(
            jnp.einsum(
                "hqk,khd->qhd",
                grad_scores,
                key_heads[:last_row],
                preferred_element_type=jnp.float32,
            )
            * HD ** (-0.5)
        )
        grad_keys = grad_keys.at[:last_row].add(
            jnp.einsum("hqk,qhd->khd", grad_scores, query_block, preferred_element_type=jnp.float32)
            * HD ** (-0.5)
        )
        grad_values = grad_values.at[:last_row].add(
            jnp.einsum(
                "hqk,qhd->khd",
                attn_probs.astype(jnp.bfloat16),
                grad_block,
                preferred_element_type=jnp.float32,
            )
        )
    return (jnp.concatenate(grad_query_parts, axis=0), grad_keys, grad_values)


def attention_part(resid_f, weights, places, segment):
    row_count = resid_f.shape[0]
    normed = compressed_norm(resid_f, weights[6].astype(jnp.float32)).astype(jnp.bfloat16)
    bias_pair = weights[4].astype(jnp.float32)
    bias_row = jnp.concatenate([bias_pair[:D], jnp.zeros((D,), jnp.float32), bias_pair[D:]])
    qkv_low = (jnp.dot(normed, weights[0], preferred_element_type=jnp.float32) + bias_row).astype(
        jnp.bfloat16
    )
    query_heads = qkv_low[:, :D].reshape(row_count, H, HD)
    key_heads = qkv_low[:, D : 2 * D].reshape(row_count, H, HD)
    value_heads = qkv_low[:, 2 * D :].reshape(row_count, H, HD)
    mixed_heads, log_sums = attend_forward(query_heads, key_heads, value_heads, places, segment)
    mixed_low = mixed_heads.reshape(row_count, D).astype(jnp.bfloat16)
    return (normed, query_heads, key_heads, value_heads, mixed_low, log_sums)


def mlp_part(middle, weights):
    normed_mlp = compressed_norm(middle, weights[7].astype(jnp.float32)).astype(jnp.bfloat16)
    pre_act = jnp.dot(normed_mlp, weights[2], preferred_element_type=jnp.float32) + weights[
        5
    ].astype(jnp.float32)
    activated = jax.nn.gelu(pre_act, approximate=True).astype(jnp.bfloat16)
    return (normed_mlp, pre_act, activated)


def on_device(
    resid,
    gain_attn,
    qkv_weight,
    qv_bias,
    out_weight,
    out_bias,
    gain_mlp,
    up_weight,
    up_bias,
    down_weight,
    down_bias,
    cotangent,
    seq_lengths,
):
    shards = (qkv_weight, out_weight, up_weight, down_weight, qv_bias, up_bias, gain_attn, gain_mlp)
    gathered = (
        lax.all_gather(shards[0], ("wide", "narrow"), axis=0, tiled=True),
        lax.all_gather(shards[1], ("wide", "narrow"), axis=0, tiled=True),
        lax.all_gather(shards[2], ("wide", "narrow"), axis=0, tiled=True),
        lax.all_gather(shards[3], ("wide", "narrow"), axis=0, tiled=True),
        lax.all_gather(shards[4], ("wide", "narrow"), axis=0, tiled=True),
        lax.all_gather(shards[5], ("wide", "narrow"), axis=0, tiled=True),
        lax.all_gather(shards[6], ("wide", "narrow"), axis=0, tiled=True),
        lax.all_gather(shards[7], ("wide", "narrow"), axis=0, tiled=True),
    )
    row_count = resid.shape[0]
    places, segment = segment_ids(seq_lengths[0], row_count)
    resid_f = resid.astype(jnp.float32)
    attn_first = attention_part(resid_f, gathered, places, segment)
    middle = (
        resid_f
        + jnp.dot(attn_first[4], gathered[1], preferred_element_type=jnp.float32)
        + out_bias.astype(jnp.float32)
    )
    mlp_first = mlp_part(middle, gathered)
    out_resid = (
        middle
        + jnp.dot(mlp_first[2], gathered[3], preferred_element_type=jnp.float32)
        + down_bias.astype(jnp.float32)
    ).astype(jnp.bfloat16)
    weights_back = (
        lax.all_gather(shards[0], ("wide", "narrow"), axis=0, tiled=True),
        lax.all_gather(shards[1], ("wide", "narrow"), axis=0, tiled=True),
        lax.all_gather(shards[2], ("wide", "narrow"), axis=0, tiled=True),
        lax.all_gather(shards[3], ("wide", "narrow"), axis=0, tiled=True),
        lax.all_gather(shards[4], ("wide", "narrow"), axis=0, tiled=True),
        lax.all_gather(shards[5], ("wide", "narrow"), axis=0, tiled=True),
        lax.all_gather(shards[6], ("wide", "narrow"), axis=0, tiled=True),
        lax.all_gather(shards[7], ("wide", "narrow"), axis=0, tiled=True),
    )
    normed_mlp, pre_act, activated = mlp_part(middle, weights_back)
    grad_out = cotangent.astype(jnp.float32)
    grad_w_down = contract_rows(activated, cotangent)
    grad_b_down = jnp.sum(grad_out, axis=0)
    grad_act = contract_cols(cotangent, weights_back[3])
    gelu_value, gelu_pull = jax.vjp(partial(jax.nn.gelu, approximate=True), pre_act)
    grad_pre = gelu_pull(grad_act)[0].astype(jnp.bfloat16)
    grad_w_up = contract_rows(normed_mlp, grad_pre)
    grad_b_up = jnp.sum(grad_pre.astype(jnp.float32), axis=0)
    grad_normed_mlp = contract_cols(grad_pre, weights_back[2])
    norm_value, norm_pull = jax.vjp(compressed_norm, middle, weights_back[7].astype(jnp.float32))
    grad_middle_norm, grad_g_mlp = norm_pull(grad_normed_mlp)
    grad_middle = grad_out + grad_middle_norm
    grad_branch = grad_middle.astype(jnp.bfloat16)
    grad_b_out = jnp.sum(grad_branch.astype(jnp.float32), axis=0)
    normed, query_heads, key_heads, value_heads, mixed_low, log_sums = attention_part(
        resid_f, weights_back, places, segment
    )
    grad_w_out = contract_rows(mixed_low, grad_branch)
    grad_mixed = (
        contract_cols(grad_branch, weights_back[1]).astype(jnp.bfloat16).reshape(row_count, H, HD)
    )
    grad_query, grad_keys, grad_values = attend_backward(
        query_heads, key_heads, value_heads, grad_mixed, log_sums, places, segment
    )
    grad_qkv = jnp.concatenate(
        [
            grad_query.reshape(row_count, D),
            grad_keys.reshape(row_count, D),
            grad_values.reshape(row_count, D),
        ],
        axis=1,
    ).astype(jnp.bfloat16)
    grad_w_qkv = contract_rows(normed, grad_qkv)
    column_sums = jnp.sum(grad_qkv.astype(jnp.float32), axis=0)
    grad_b_qv = jnp.concatenate([column_sums[:D], column_sums[2 * D :]])
    grad_normed = contract_cols(grad_qkv, weights_back[0])
    first_value, first_pull = jax.vjp(compressed_norm, resid_f, weights_back[6].astype(jnp.float32))
    grad_resid_norm, grad_g_attn = first_pull(grad_normed)
    grad_resid = (grad_middle + grad_resid_norm).astype(jnp.bfloat16)
    every_shard = (
        lax.psum_scatter(grad_w_qkv, ("wide", "narrow"), scatter_dimension=0, tiled=True),
        lax.psum_scatter(grad_w_out, ("wide", "narrow"), scatter_dimension=0, tiled=True),
        lax.psum_scatter(grad_b_qv, ("wide", "narrow"), scatter_dimension=0, tiled=True),
        lax.psum_scatter(grad_g_attn, ("wide", "narrow"), scatter_dimension=0, tiled=True),
        lax.psum_scatter(grad_w_up, ("wide", "narrow"), scatter_dimension=0, tiled=True),
        lax.psum_scatter(grad_w_down, ("wide", "narrow"), scatter_dimension=0, tiled=True),
        lax.psum_scatter(grad_b_up, ("wide", "narrow"), scatter_dimension=0, tiled=True),
        lax.psum_scatter(grad_g_mlp, ("wide", "narrow"), scatter_dimension=0, tiled=True),
    )
    attn_shards = every_shard[:4]
    mlp_shards = every_shard[4:]
    bias_sums = lax.psum((grad_b_out, grad_b_down), ("wide", "narrow"))
    return (
        out_resid,
        grad_resid,
        attn_shards[3],
        attn_shards[0],
        attn_shards[2],
        attn_shards[1],
        bias_sums[0],
        mlp_shards[3],
        mlp_shards[0],
        mlp_shards[2],
        mlp_shards[1],
        bias_sums[1],
    )


def solution(mesh):
    return jax.shard_map(
        on_device,
        mesh=mesh,
        in_specs=(
            P(("wide", "narrow"), None),
            P(("wide", "narrow")),
            P(("wide", "narrow"), None),
            P(("wide", "narrow")),
            P(("wide", "narrow"), None),
            P(),
            P(("wide", "narrow")),
            P(("wide", "narrow"), None),
            P(("wide", "narrow")),
            P(("wide", "narrow"), None),
            P(),
            P(("wide", "narrow"), None),
            P(("wide", "narrow"), None),
        ),
        out_specs=(
            P(("wide", "narrow"), None),
            P(("wide", "narrow"), None),
            P(("wide", "narrow")),
            P(("wide", "narrow"), None),
            P(("wide", "narrow")),
            P(("wide", "narrow"), None),
            P(),
            P(("wide", "narrow")),
            P(("wide", "narrow"), None),
            P(("wide", "narrow")),
            P(("wide", "narrow"), None),
            P(),
        ),
        check_vma=False,
    )
```

profile of v0, /device:TPU:0, one launch (start us, length us, event | category | flops | bytes accessed | tf_op | source)
XLA Modules:
  0.0 832.7 jit_solution(7237339441926074509)
XLA Ops:
  7.2 0.7 all-gather.5.cloned.1.call-update
  8.0 0.7 all-gather.7.cloned.1.call-update
  8.7 0.7 all-gather.9.cloned.1.call-update
  10.1 1.7 copy.76
  11.9 1.1 copy-done.8
  13.3 1.8 convert_element_type.99
  16.4 42.5 %all-reduce.11 = (bf16[1536]{0:T(1024)(128)(2,1)S(1)}, bf16[768]{0:T(1024)(128)(2,1)S(1)}, bf16[768]{0:T(1024)(128)(2,1)S(1)}, bf16[3072]{0:T(1024)(128)(2,1)S(1)}) all-reduce(bf16[1536]{0:T(1024)(128)(2,1)S(1)} %dynamic-update-slice.11, ...), channel_id=1, replica_groups=mesh['wide'=8,'narrow'=4] {'wide','narrow'}, use_global_device_ids=true, to_apply=%add.3 | all-reduce | flops 6144 | bytes 24576
  59.6 2.6 copy.85
  63.3 1.4 fusion.25
  64.8 9.1 %all-gather.5.cloned.1.call-done = bf16[768,2304]{1,0:T(8,128)(2,1)} async-done(((bf16[24,2304]{1,0:T(8,128)(2,1)}), bf16[768,2304]{1,0:T(8,128)(2,1)}) %all-gather.5.cloned.1.call-update) | async-done | bytes 3538960 | tf_op jit(solution)/shard_map/all_gather | solution.py:164
  73.8 6.3 add_convert_fusion
  80.2 1.7 fusion.54
  81.9 1.9 fusion.55
  83.8 1.8 copy.83
  85.6 2.0 copy.79
  87.6 2.6 copy.82
  90.2 2.3 copy.78
  92.5 12.0 %fusion.15 = (f32[12,512]{1,0:T(8,128)S(1)}, f32[12,512,1024]{2,1,0:T(8,128)}) fusion(pred[512,1024]{1,0:T(8,128)(4,1)S(1)} %copy-done.10, bf16[512,12,64]{0,2,1:T(8,128)(2,1)} %bitcast.80, bf16[1024,12,64]{0,2,1:T(8,128)(2,1)S(1)} %bitcast.76), kind=kOutput, calls=%fused_computation.32 | convolution fusion | flops 824174592 | bytes 28073984 | tf_op jit(solution)/shard_map/qhd,khd->hqk/dot_general | solution.py:44
  104.5 12.1 %fusion = f32[12,512]{1,0:T(8,128)S(1)} fusion(f32[12,512]{1,0:T(8,128)S(1)} %get-tuple-element.156, f32[12,512,1024]{2,1,0:T(8,128)} %get-tuple-element.157, pred[512,1024]{1,0:T(8,128)(4,1)S(1)} %copy-done.10), kind=kLoop, calls=%fused_computation.6 | loop fusion | flops 25159680 | bytes 25739264 | tf_op jit(solution)/shard_map/reduce_sum | solution.py:66
  116.6 2.1 fusion.20
  118.7 2.6 fusion.13
  121.3 2.0 copy-done
  123.6 2.0 copy.81
  125.6 7.3 fusion.37
  132.9 12.0 %fusion.36 = bf16[512,12,64]{0,2,1:T(8,128)(2,1)S(1)} fusion(bf16[1024,12,64]{0,2,1:T(8,128)(2,1)S(1)} %bitcast.87, f32[12,512]{1,0:T(8,128)S(1)} %fusion, f32[12,512]{1,0:T(8,128)S(1)} %get-tuple-element.156, f32[12,512,1024]{2,1,0:T(8,128)} %get-tuple-element.157, pred[512,1024]{1,0:T(8,128)(4,1)S(1)} %copy-done.10), kind=kOutput, calls=%fused_computation.78 | convolution fusion | flops 837156864 | bytes 28098560 | tf_op jit(solution)/shard_map/hqk,khd->qhd/dot_general | solution.py:69
  145.0 1.3 pad_maximum_fusion.3
  146.3 3.8 fusion.60
  150.5 44.6 %all-gather.9.cloned.1.call-done = bf16[768,3072]{1,0:T(8,128)(2,1)} async-done(((bf16[24,3072]{1,0:T(8,128)(2,1)}), bf16[768,3072]{1,0:T(8,128)(2,1)}) %all-gather.9.cloned.1.call-update) | async-done | bytes 4718608 | tf_op jit(solution)/shard_map/all_gather | solution.py:166
  195.1 10.9 %fusion.51 = f32[1024,3072]{1,0:T(8,128)} fusion(bf16[768,3072]{1,0:T(8,128)(2,1)} %all-gather.9.cloned.1.call-done, f32[768]{0:T(1024)S(1)} %convert_element_type.109, f32[1024]{0:T(1024)S(1)} %fusion.39, f32[1024,1]{0,1:T(1,128)S(1)} %bitcast.104, f32[1024,767]{0,1:T(8,128)S(1)} %get-tuple-element.161), kind=kOutput, calls=%fused_computation.106 | convolution fusion | flops 4834983936 | bytes 20454400 | tf_op jit(solution)/shard_map/dot_general | solution.py:140
  206.0 54.3 %all-gather.11.cloned.1.call-done = bf16[3072,767]{1,0:T(8,128)(2,1)} async-done(((bf16[96,767]{1,0:T(8,128)(2,1)}), bf16[3072,767]{1,0:T(8,128)(2,1)}) %all-gather.11.cloned.1.call-update) | async-done | bytes 4712464 | tf_op jit(solution)/shard_map/all_gather | solution.py:167
  260.4 17.2 %convert_reduce_fusion = (f32[3072]{0:T(1024)}, bf16[1024,3072]{1,0:T(8,128)(2,1)S(1)}) fusion(f32[1024,3072]{1,0:T(8,128)} %fusion.51, f32[3072]{0:T(1024)S(1)} %copy-done.44, bf16[1024,767]{1,0:T(8,128)(2,1)} %param.36, bf16[3072,767]{1,0:T(8,128)(2,1)} %all-gather.11.cloned.1.call-done), kind=kOutput, calls=%fused_computation.18 | convolution fusion | flops 4897895424 | bytes 25182208 | tf_op jit(solution)/shard_map/dot_general | solution.py:31
  277.6 6.0 multiply_reduce_fusion.2
  283.6 0.7 add_add_fusion.1
  284.3 1.6 copy-done.1
  285.9 1.1 convert_reduce_fusion.3
  287.0 2.9 fusion.61
  289.9 1.4 convolution_convert_fusion
  291.5 7.7 fusion.29
  299.2 6.9 multiply_reduce_fusion.1
  306.1 7.2 multiply_convert_fusion.1
  313.4 2.0 fusion.35
  315.4 3.1 multiply_bitcast_fusion
  318.6 21.5 %multiply_reduce_fusion = (f32[12,512]{1,0:T(8,128)S(1)}, f32[12,512,1024]{2,1,0:T(8,128)}) fusion(f32[12,512]{1,0:T(8,128)S(1)} %log_add_fusion, f32[12,512,1024]{2,1,0:T(8,128)} %get-tuple-element.157, pred[512,1024]{1,0:T(8,128)(4,1)S(1)} %copy-done.11, bf16[512,12,64]{0,2,1:T(8,128)(2,1)S(1)} %bitcast.96, bf16[1024,12,64]{0,2,1:T(8,128)(2,1)S(1)} %bitcast.88), kind=kOutput, calls=%fused_computation.1 | convolution fusion | flops 836757504 | bytes 53264384 | tf_op jit(solution)/shard_map/qhd,khd->hqk/dot_general | solution.py:93
  340.1 17.8 %multiply_convert_fusion = bf16[12,512,1024]{2,1,0:T(8,128)(2,1)S(1)} fusion(f32[12,512,1024]{2,1,0:T(8,128)} %get-tuple-element.166, f32[12,512]{1,0:T(8,128)S(1)} %get-tuple-element.165, f32[12,512]{1,0:T(8,128)S(1)} %log_add_fusion, f32[12,512,1024]{2,1,0:T(8,128)} %get-tuple-element.157, pred[512,1024]{1,0:T(8,128)(4,1)} %fusion.25), kind=kLoop, calls=%fused_computation | loop fusion | flops 37748736 | bytes 63488000 | tf_op jit(solution)/shard_map/convert_element_type | solution.py:97
  357.9 6.3 fusion.34
  364.3 2.7 pad_maximum_fusion.4
  367.0 5.2 fusion.24
  372.2 13.2 %fusion.23 = bf16[1024,12,64]{0,2,1:T(8,128)(2,1)S(1)} fusion(f32[512,12,64]{0,2,1:T(8,128)} %fusion.29, bf16[512,12,64]{0,2,1:T(8,128)(2,1)} %bitcast.97, f32[12,512]{1,0:T(8,128)S(1)} %log_add_fusion, f32[12,512,1024]{2,1,0:T(8,128)} %get-tuple-element.157, pred[512,1024]{1,0:T(8,128)(4,1)S(1)} %copy-done.12), kind=kOutput, calls=%fused_computation.49 | convolution fusion | flops 832045056 | bytes 29646848 | tf_op jit(solution)/shard_map/hqk,qhd->khd/dot_general | solution.py:112
  385.4 1.2 copy-done.29
  386.6 6.8 fusion.48
  393.5 13.3 %fusion.52 = f32[3072,767]{1,0:T(8,128)} fusion(bf16[1024,767]{1,0:T(8,128)(2,1)} %param.36, f32[1024,3072]{1,0:T(8,128)} %fusion.51, f32[3072]{0:T(1024)S(1)} %copy-done.44), kind=kOutput, calls=%fused_computation.107 | convolution fusion | flops 4857004032 | bytes 23590912 | tf_op jit(solution)/shard_map/dot_general | solution.py:25
  406.9 10.6 %fusion.50 = f32[768,3072]{1,0:T(8,128)} fusion(bf16[1024,3072]{1,0:T(8,128)(2,1)} %copy-done.55, f32[768]{0:T(1024)S(1)} %convert_element_type.109, f32[1024]{0:T(1024)S(1)} %fusion.39, f32[1024,1]{0,1:T(1,128)S(1)} %bitcast.107, f32[1024,767]{0,1:T(8,128)} %copy-done.5), kind=kOutput, calls=%fused_computation.105 | convolution fusion | flops 4834983936 | bytes 18881536 | tf_op jit(solution)/shard_map/dot_general | solution.py:25
  417.5 0.7 copy-done.48
  418.2 12.2 %add_convert_fusion.1 = bf16[1024,767]{0,1:T(8,128)(2,1)} fusion(f32[1024,767]{0,1:T(8,128)} %copy-done.5, bf16[3072,767]{1,0:T(8,128)(2,1)} %all-gather.11.cloned.1.call-done, f32[767]{0:T(1024)S(1)} %convert_element_type.113, f32[1024,3072]{1,0:T(8,128)} %fusion.51, f32[3072]{0:T(1024)S(1)} %copy-done.44), kind=kOutput, calls=%fused_computation.57 | convolution fusion | flops 4859360256 | bytes 22023164 | tf_op jit(solution)/shard_map/dot_general | solution.py:185
  430.4 2.6 copy.89
  433.0 3.0 convert_reduce_fusion.1
  437.1 6.3 multiply_reduce_fusion.3
  444.1 1.3 copy-done.2
  446.0 0.8 convert_reduce_fusion.2
  446.8 41.9 %all-reduce.10 = (f32[768]{0:T(1024)S(1)}, f32[1536]{0:T(1024)S(1)}, f32[767]{0:T(1024)}, f32[768]{0:T(1024)S(1)}, f32[3072]{0:T(1024)S(1)}, /*index=5*/f32[767]{0:T(1024)}) all-reduce(f32[768]{0:T(1024)S(1)} %get-tuple-element.126, f32[1536]{0:T(1024)S(1)} %pad_maximum_fusion.6, ...), channel_id=2, replica_groups=mesh['wide'=8,'narrow'=4] {'wide','narrow'}, use_global_device_ids=true, to_apply=%region_15.16.clone | all-reduce | flops 7678 | bytes 61424
  489.9 1.6 copy.90
  492.6 49.7 %reduce-scatter.5.cloned.1.call-done = f32[24,2304]{1,0:T(8,128)} async-done(((f32[768,2304]{1,0:T(8,128)}), f32[24,2304]{1,0:T(8,128)}) %reduce-scatter.5.cloned.1.call-update) | async-done | bytes 221200 | tf_op jit(solution)/shard_map/reduce_scatter | solution.py:239
  542.3 141.4 %reduce-scatter.11.cloned.1.call-done = f32[96,767]{1,0:T(8,128)} async-done(((f32[3072,767]{1,0:T(8,128)}), f32[96,767]{1,0:T(8,128)}) %reduce-scatter.11.cloned.1.call-update) | async-done | bytes 294544 | tf_op jit(solution)/shard_map/reduce_scatter | solution.py:244
  683.6 142.1 %reduce-scatter.9.cloned.1.call-done = f32[24,3072]{1,0:T(8,128)} async-done(((f32[768,3072]{1,0:T(8,128)}), f32[24,3072]{1,0:T(8,128)}) %reduce-scatter.9.cloned.1.call-update) | async-done | bytes 294928 | tf_op jit(solution)/shard_map/reduce_scatter | solution.py:243
  (174 shorter events, 9.7 us)
Async XLA Ops:
  7.2 66.7 %all-gather.5.cloned.1.call-start = ((), (), s32[]{:S(2)}) async-start(), calls=%async_computation.4 | async-start | bytes 3649536 | tf_op jit(solution)/shard_map/all_gather | solution.py:164
  7.9 138.4 %all-gather.7.cloned.1.call-start = ((), (), s32[]{:S(2)}) async-start(), calls=%async_computation.5 | async-start | bytes 1216512 | tf_op jit(solution)/shard_map/all_gather | solution.py:165
  8.7 186.5 %all-gather.9.cloned.1.call-start = ((), (), s32[]{:S(2)}) async-start(), calls=%async_computation.6 | async-start | bytes 4866048 | tf_op jit(solution)/shard_map/all_gather | solution.py:166
  9.4 251.0 %all-gather.11.cloned.1.call-start = ((), (), s32[]{:S(2)}) async-start(), calls=%async_computation.7 | async-start | bytes 4866048 | tf_op jit(solution)/shard_map/all_gather | solution.py:167
  10.0 482.6 %reduce-scatter.7.cloned.1.call-start = ((), (), s32[]{:S(2)}) async-start(), calls=%async_computation.9 | async-start | bytes 2433024 | tf_op jit(solution)/shard_map/reduce_scatter | solution.py:240
  10.0 5.0 copy-start.50
  10.0 5.3 copy-start.47
  10.0 5.4 copy-start.51
  10.1 5.6 copy-start.52
  10.1 5.9 copy-start.53
  10.1 6.1 copy-start.54
  11.8 1.1 copy-start.8
  15.1 65.1 %copy-start.3 = (f32[1024,767]{0,1:T(8,128)}, f32[1024,767]{0,1:T(8,128)S(1)}, u32[]{:S(2)}) copy-start(f32[1024,767]{0,1:T(8,128)S(1)} %convert_element_type.99) | copy-start | bytes 9424900
  59.0 21.2 %copy-start.40 = (f32[768]{0:T(1024)}, f32[768]{0:T(1024)S(1)}, u32[]{:S(2)}) copy-start(f32[768]{0:T(1024)S(1)} %convert_element_type.100) | copy-start | bytes 9220
  59.6 20.6 %copy-start.35 = (f32[1024]{0:T(1024)}, f32[1024]{0:T(1024)S(1)}, u32[]{:S(2)}) copy-start(f32[1024]{0:T(1024)S(1)} %neg.38) | copy-start | bytes 12292
  63.1 17.2 %copy-start.42 = (f32[1024]{0:T(1024)}, f32[1024]{0:T(1024)S(1)}, u32[]{:S(2)}) copy-start(f32[1024]{0:T(1024)S(1)} %fusion.38) | copy-start | bytes 12292
  83.8 8.7 %copy-start.10 = (pred[512,1024]{1,0:T(8,128)(4,1)S(1)}, pred[512,1024]{1,0:T(8,128)(4,1)}, u32[]{:S(2)}) copy-start(pred[512,1024]{1,0:T(8,128)(4,1)} %fusion.25) | copy-start | bytes 1572868
  85.6 18.9 %copy-start.9 = (bf16[1024,768]{0,1:T(8,128)(2,1)}, bf16[1024,768]{0,1:T(8,128)(2,1)S(1)}, u32[]{:S(2)}) copy-start(bf16[1024,768]{0,1:T(8,128)(2,1)S(1)} %copy.83) | copy-start | bytes 4718596
  87.6 29.0 %copy-start.13 = (bf16[512,768]{0,1:T(8,128)(2,1)}, bf16[512,768]{0,1:T(8,128)(2,1)S(1)}, u32[]{:S(2)}) copy-start(bf16[512,768]{0,1:T(8,128)(2,1)S(1)} %copy.79) | copy-start | bytes 2359300
  104.5 12.1 %copy-start.17 = (bf16[512,768]{0,1:T(8,128)(2,1)S(1)}, bf16[512,768]{0,1:T(8,128)(2,1)}, u32[]{:S(2)}) copy-start(bf16[512,768]{0,1:T(8,128)(2,1)} %copy.78) | copy-start | bytes 2359300
  118.7 4.6 copy-start
  118.7 4.6 copy-start.26
  123.3 9.6 %copy-start.31 = (f32[12,512]{1,0:T(8,128)}, f32[12,512]{1,0:T(8,128)S(1)}, u32[]{:S(2)}) copy-start(f32[12,512]{1,0:T(8,128)S(1)} %fusion.13) | copy-start | bytes 73732
  123.6 9.3 %copy-start.24 = (bf16[512,768]{0,1:T(8,128)(2,1)}, bf16[512,768]{0,1:T(8,128)(2,1)S(1)}, u32[]{:S(2)}) copy-start(bf16[512,768]{0,1:T(8,128)(2,1)S(1)} %copy.77) | copy-start | bytes 2359300
  125.6 7.3 copy-start.19
  146.3 4.1 copy-start.32
  150.1 133.4 %copy-start.5 = (f32[1024,767]{0,1:T(8,128)}, f32[1024,767]{0,1:T(8,128)S(1)}, u32[]{:S(2)}) copy-start(f32[1024,767]{0,1:T(8,128)S(1)} %get-tuple-element.161) | copy-start | bytes 9424900
  150.5 109.9 %copy-start.44 = (f32[3072]{0:T(1024)S(1)}, f32[3072]{0:T(1024)}, u32[]{:S(2)}) copy-start(f32[3072]{0:T(1024)} %convert_element_type.111) | copy-start | bytes 36868
  260.4 17.2 %copy-start.23 = (bf16[768,3072]{1,0:T(8,128)(2,1)S(1)}, bf16[768,3072]{1,0:T(8,128)(2,1)}, u32[]{:S(2)}) copy-start(bf16[768,3072]{1,0:T(8,128)(2,1)} %all-gather.9.cloned.1.call-done) | copy-start | bytes 14155780
  277.6 6.0 copy-start.55
  283.6 2.3 copy-start.6
  284.3 1.6 copy-start.1
  284.3 2.8 copy-start.28
  284.3 5.6 copy-start.33
  287.0 2.9 copy-start.49
  289.9 9.3 %slice-start = ((s8[12582912]{0:T(1024)(128)(4,1)}), s8[4194304]{0:T(1024)(128)(4,1)S(1)}, s32[]{:S(2)}) async-start(s8[12582912]{0:T(1024)(128)(4,1)} %bitcast.74), calls=%async_computation.12 | async-start | bytes 8388608
  291.3 7.9 slice-start.1
  291.5 27.2 %copy-start.27 = (bf16[512,768]{0,1:T(8,128)(2,1)}, bf16[512,768]{0,1:T(8,128)(2,1)S(1)}, u32[]{:S(2)}) copy-start(bf16[512,768]{0,1:T(8,128)(2,1)S(1)} %get-tuple-element.148) | copy-start | bytes 2359300
  291.5 7.7 slice-start.2
  291.5 7.7 copy-start.25
  306.1 7.2 copy-start.14
  313.4 2.0 copy-start.18
  315.4 3.2 copy-start.11
  315.4 3.2 copy-start.20
  318.6 223.7 %reduce-scatter.5.cloned.1.call-start = ((), (), s32[]{:S(2)}) async-start(), calls=%async_computation.8 | async-start | bytes 7299072 | tf_op jit(solution)/shard_map/reduce_scatter | solution.py:239
  367.0 5.2 copy-start.12
  372.1 14.4 %copy-start.4 = (f32[1024,767]{0,1:T(8,128)S(1)}, f32[1024,767]{0,1:T(8,128)}, u32[]{:S(2)}) copy-start(f32[1024,767]{0,1:T(8,128)} %copy-done.3) | copy-start | bytes 9424900
  372.1 14.4 %copy-start.15 = (bf16[1024,12,64]{0,2,1:T(8,128)(2,1)S(1)}, bf16[1024,12,64]{0,2,1:T(8,128)(2,1)}, u32[]{:S(2)}) copy-start(bf16[1024,12,64]{0,2,1:T(8,128)(2,1)} %fusion.24) | copy-start | bytes 4718596
  372.1 14.4 %copy-start.21 = (bf16[1024,12,64]{0,2,1:T(8,128)(2,1)S(1)}, bf16[1024,12,64]{0,2,1:T(8,128)(2,1)}, u32[]{:S(2)}) copy-start(bf16[1024,12,64]{0,2,1:T(8,128)(2,1)} %pad_maximum_fusion.4) | copy-start | bytes 4718596
  372.1 14.4 %copy-start.36 = (f32[1024]{0:T(1024)S(1)}, f32[1024]{0:T(1024)}, u32[]{:S(2)}) copy-start(f32[1024]{0:T(1024)} %copy-done.35) | copy-start | bytes 12292
  372.2 14.4 %copy-start.41 = (f32[768]{0:T(1024)S(1)}, f32[768]{0:T(1024)}, u32[]{:S(2)}) copy-start(f32[768]{0:T(1024)} %copy-done.40) | copy-start | bytes 9220
  372.2 14.4 %copy-start.43 = (f32[1024]{0:T(1024)S(1)}, f32[1024]{0:T(1024)}, u32[]{:S(2)}) copy-start(f32[1024]{0:T(1024)} %copy-done.42) | copy-start | bytes 12292
  385.4 1.2 copy-start.29
  393.4 290.2 %reduce-scatter.11.cloned.1.call-start = ((), (), s32[]{:S(2)}) async-start(), calls=%async_computation.11 | async-start | bytes 9732096 | tf_op jit(solution)/shard_map/reduce_scatter | solution.py:244
  406.8 418.9 %reduce-scatter.9.cloned.1.call-start = ((), (), s32[]{:S(2)}) async-start(), calls=%async_computation.10 | async-start | bytes 9732096 | tf_op jit(solution)/shard_map/reduce_scatter | solution.py:243
  433.0 3.1 copy-start.16
  433.0 3.6 copy-start.22
  433.0 4.1 copy-start.30
  437.1 6.3 copy-start.38
  443.4 2.0 copy-start.2
  443.4 2.5 copy-start.7
  443.5 2.5 copy-start.34
  446.0 0.8 copy-start.45
  446.0 0.8 copy-start.46
  (3 other events, 2.0 us)
Sparse Core Ops, SparseCore 0:
  10.9 62.8 all-gather.4
  76.7 52.8 all-gather.6
  132.5 62.5 all-gather.8
  197.9 62.4 all-gather.10
  318.7 97.8 reduce-scatter.6
  423.6 118.5 reduce-scatter.4
  548.7 134.8 reduce-scatter.10
  691.1 134.5 reduce-scatter.8
where the time goes:
time: 836 us; the launch traced here: 833 us
  waiting for transfers between devices  444 us (53%)
  matrix products  197 us (24%)
  blocking collectives  84.5 us (10%)
  other arithmetic  55.2 us (7%)
  local copies, waits for them, and re-layouts  36.7 us (4%)
  between operations  15.2 us (2%)
    reduce_scatter x1, waiting for transfers between devices, on_device(): lax.psum_scatter(grad_w_up, ('wide', 'narrow'), scatter_dimension=0, tile...  142 us
    reduce_scatter x1, waiting for transfers between devices, on_device(): lax.psum_scatter(grad_w_down, ('wide', 'narrow'), scatter_dimension=0, ti...  141 us
    unnamed x2, blocking collectives  84.5 us
    all_gather x1, waiting for transfers between devices, on_device(): lax.all_gather(shards[3], ('wide', 'narrow'), axis=0, tiled=True)  54.3 us
    reduce_scatter x1, waiting for transfers between devices, on_device(): lax.psum_scatter(grad_w_qkv, ('wide', 'narrow'), scatter_dimension=0, til...  49.7 us
    all_gather x1, waiting for transfers between devices, on_device(): lax.all_gather(shards[2], ('wide', 'narrow'), axis=0, tiled=True)  44.6 us
    dot_general x4, matrix products, contract_rows(): lax.dot_general(left_side, right_side, (((0,), (0,)), ((), ())), preferre...  33.7 us
    dot_general x4, matrix products, contract_cols(): lax.dot_general(left_side, right_side, (((1,), (1,)), ((), ())), preferre...  30.9 us
  transfers between devices with their start and end apart: 8, of which 6 were waited for; matrix products, arithmetic and copies ran while one was open for 27% of the time, Pallas kernels for 0%

commit v1 on v0

--- a/solution.py
+++ b/solution.py
@@ -3,6 +3,8 @@
 import jax
 import jax.numpy as jnp
 from jax import lax
+from jax.experimental import pallas as pl
+from jax.experimental.pallas import tpu as pltpu
 from jax.sharding import PartitionSpec as P
 
 D = 768
@@ -144,7 +146,564 @@
     return (normed_mlp, pre_act, activated)
 
 
+MESH = pl.DeviceIdType.MESH
+ZF, ZN, Y, X, CORE = range(5)
+CHIP_AXES = 4
+BLOCK = 48
+
+
+class Place:
+    def __init__(self):
+        wide = lax.axis_index("wide")
+        narrow = lax.axis_index("narrow")
+        self.wide, self.narrow = wide, narrow
+        self.bits = (
+            lax.div(wide, 4),
+            lax.rem(lax.div(wide, 2), 2),
+            lax.rem(wide, 2),
+            lax.div(narrow, 2),
+            lax.rem(narrow, 2),
+        )
+
+    def other(self, axis):
+        flip = 1 - 2 * self.bits[axis]
+        if axis == X:
+            return (self.wide, self.narrow + 2 * flip)
+        if axis == CORE:
+            return (self.wide, self.narrow + flip)
+        return (self.wide + (4, 2, 1)[axis] * flip, self.narrow)
+
+    def region(self, full, flipped):
+        return tuple(
+            pl.ds(0, 2)
+            if axis in full
+            else (1 - self.bits[axis] if axis in flipped else self.bits[axis])
+            for axis in range(CHIP_AXES)
+        )
+
+
+def enter(place, axes):
+    barrier = pltpu.get_barrier_semaphore()
+    for axis in axes:
+        pl.semaphore_signal(
+            barrier, inc=1, device_id=place.other(axis), device_id_type=MESH
+        )
+    pl.semaphore_wait(barrier, len(axes))
+
+
+def send(place, axis, src, dst, send_sem, recv_sem):
+    return pltpu.make_async_remote_copy(
+        src_ref=src,
+        dst_ref=dst,
+        send_sem=send_sem,
+        recv_sem=recv_sem,
+        device_id=place.other(axis),
+        device_id_type=MESH,
+    )
+
+
+GATHER_COPIES = 15
+
+
+def pair_index(stage, piece):
+    return stage * (stage - 1) // 2 + piece
+
+
+class GatherChunk:
+    def __init__(self, place, order, view, own, send_sems, recv_sems):
+        self.place, self.order, self.view, self.own = place, order, view, own
+        self.send_sems, self.recv_sems = send_sems, recv_sems
+        self.started = []
+
+    def piece_region(self, piece, flipped=()):
+        full = self.order[: max(piece - 1, 0)]
+        turned = ((self.order[piece - 1],) if piece else ()) + tuple(flipped)
+        return self.place.region(full, turned)
+
+    def copy(self, stage, piece):
+        axis = (self.order + (CORE,))[stage - 1]
+        core = self.place.bits[CORE]
+        here = self.view(self.piece_region(piece), core)
+        src = self.own if piece == 0 else here
+        slot = pair_index(stage, piece)
+        return send(
+            self.place, axis, src, here, self.send_sems.at[slot], self.recv_sems.at[slot]
+        )
+
+    def arrival(self, stage, piece):
+        axis = (self.order + (CORE,))[stage - 1]
+        core = self.place.bits[CORE]
+        if axis == CORE:
+            there = self.view(self.piece_region(piece), 1 - core)
+        else:
+            there = self.view(self.piece_region(piece, (axis,)), core)
+        slot = pair_index(stage, piece)
+        return send(
+            self.place, axis, there, there, self.send_sems.at[slot], self.recv_sems.at[slot]
+        )
+
+    def start(self, piece):
+        for stage in range(piece + 1, CHIP_AXES + 2):
+            copy = self.copy(stage, piece)
+            copy.start()
+            self.started.append(copy)
+
+    def step(self, stage):
+        if stage:
+            for piece in range(stage):
+                self.arrival(stage, piece).wait_recv()
+        if stage <= CHIP_AXES:
+            self.start(stage)
+
+    def drain(self):
+        for copy in self.started:
+            copy.wait_send()
+
+
+def sum_small(place, steps, send_sems, recv_sems, first, count):
+    values, landing = steps
+    axis = first
+    copy = send(
+        place, axis, values.at[count], landing.at[count], send_sems.at[count], recv_sems.at[count]
+    )
+    return copy
+
+
+def gather_kernel(
+    qkv_in, out_in, up_in, down_in, small_in,
+    qkv_w, out_w, up_w, down_w, small_out,
+    pair_f32, pair_low, small_values, small_landing,
+    pair_send, pair_recv, own_sems, small_send, small_recv, send_sems, recv_sems,
+):
+    place = Place()
+    core = place.bits[CORE]
+    enter(place, range(5))
+    widths = (qkv_in.shape[1], out_in.shape[1], up_in.shape[1])
+    offsets = (0, widths[0], widths[0] + widths[1])
+    rows = qkv_in.shape[0]
+    small_values[0] = small_in[...]
+
+    def small_copy(count):
+        return send(
+            place, count, small_values.at[count], small_landing.at[count],
+            small_send.at[count], small_recv.at[count],
+        )
+
+    pair_copies = []
+    own_rows = pl.ds(pl.multiple_of(core * rows, 8), rows)
+    for slot, (shard, offset, width) in enumerate(zip((qkv_in, out_in, up_in), offsets, widths)):
+        copy = send(
+            place, CORE, shard, pair_f32.at[own_rows, pl.ds(offset, width)],
+            pair_send.at[slot], pair_recv.at[slot],
+        )
+        copy.start()
+        pair_copies.append(copy)
+    small_copy(0).start()
+    for shard, offset, width in zip((qkv_in, out_in, up_in), offsets, widths):
+        pair_f32[own_rows, pl.ds(offset, width)] = shard[...]
+
+    chunks = []
+    own_copies = []
+    for slot, (whole, offset, width) in enumerate(zip((qkv_w, out_w, up_w), offsets, widths)):
+        pair_copies[slot].wait()
+        pair_low[:, pl.ds(offset, width)] = pair_f32[:, pl.ds(offset, width)].astype(jnp.bfloat16)
+        half = width // 2
+        first = -(-half // 256) * 128
+        here = place.region((), ())
+        own_copy = pltpu.make_async_copy(
+            pair_low.at[:, pl.ds(pl.multiple_of(offset + core * half, 128), half)],
+            whole.at[here + (pl.ds(0, BLOCK), pl.ds(pl.multiple_of(core * half, 128), half))],
+            own_sems.at[slot],
+        )
+        own_copy.start()
+        own_copies.append(own_copy)
+        for order, start, count in (
+            ((ZF, ZN, Y, X), 0, first),
+            ((ZF, ZN, X, Y), first, half - first),
+        ):
+            def view(region, bit, whole=whole, half=half, start=start, count=count):
+                return whole.at[
+                    region
+                    + (pl.ds(0, BLOCK), pl.ds(pl.multiple_of(bit * half + start, 128), count))
+                ]
+
+            own = pair_low.at[:, pl.ds(pl.multiple_of(offset + core * half + start, 128), count)]
+            index = len(chunks)
+            chunks.append(
+                GatherChunk(place, order, view, own, send_sems.at[index], recv_sems.at[index])
+            )
+            chunks[-1].step(0)
+    own_copy = pltpu.make_async_copy(
+        down_in, down_w.at[place.region((), ()) + (core,)], own_sems.at[3]
+    )
+    own_copy.start()
+    own_copies.append(own_copy)
+    half = down_in.shape[1] // 2
+    for order, start in (((ZF, ZN, Y, X), 0), ((ZF, ZN, X, Y), half)):
+        def view(region, bit, start=start):
+            return down_w.at[region + (bit, pl.ds(0, down_in.shape[0]), pl.ds(start, half))]
+
+        own = down_in.at[:, pl.ds(start, half)]
+        index = len(chunks)
+        chunks.append(
+            GatherChunk(place, order, view, own, send_sems.at[index], recv_sems.at[index])
+        )
+        chunks[-1].step(0)
+
+    for count in range(5):
+        small_copy(count).wait()
+        small_values[count + 1] = small_values[count] + small_landing[count]
+        if count < 4:
+            small_copy(count + 1).start()
+    small_out[...] = small_values[5]
+
+    for slot in range(4 + 4):
+        for tensor in range(4):
+            stage = slot - tensor + 1
+            if 1 <= stage <= 5:
+                chunks[2 * tensor].step(stage)
+                chunks[2 * tensor + 1].step(stage)
+    for own_copy in own_copies:
+        own_copy.wait()
+    for chunk in chunks:
+        chunk.drain()
+
+
+def gather_weights(qkv_in, out_in, up_in, down_in, small_in):
+    rows = qkv_in.shape[0]
+    widths = (qkv_in.shape[1], out_in.shape[1], up_in.shape[1])
+    grid = (2, 2, 2, 2)
+    outs = [
+        jax.ShapeDtypeStruct(grid + (BLOCK, width), jnp.bfloat16) for width in widths
+    ] + [
+        jax.ShapeDtypeStruct(grid + (2,) + down_in.shape, jnp.bfloat16),
+        jax.ShapeDtypeStruct(small_in.shape, jnp.float32),
+    ]
+    in_vmem = pl.BlockSpec(memory_space=pltpu.VMEM)
+    in_hbm = pl.BlockSpec(memory_space=pl.ANY)
+    dma = pltpu.SemaphoreType.DMA
+    results = pl.pallas_call(
+        gather_kernel,
+        out_shape=outs,
+        in_specs=[in_vmem] * 5,
+        out_specs=[in_hbm] * 4 + [in_vmem],
+        scratch_shapes=[
+            pltpu.VMEM((BLOCK, sum(widths)), jnp.float32),
+            pltpu.VMEM((BLOCK, sum(widths)), jnp.bfloat16),
+            pltpu.VMEM((6,) + small_in.shape, jnp.float32),
+            pltpu.VMEM((5,) + small_in.shape, jnp.float32),
+            dma((3,)),
+            dma((3,)),
+            dma((4,)),
+            dma((5,)),
+            dma((5,)),
+            dma((8, GATHER_COPIES)),
+            dma((8, GATHER_COPIES)),
+        ],
+        compiler_params=pltpu.CompilerParams(
+            collective_id=1, has_side_effects=True, vmem_limit_bytes=48 * 2**20
+        ),
+        name="gather_weights",
+    )(qkv_in, out_in, up_in, down_in, small_in)
+    return [
+        results[0].reshape(-1, widths[0]),
+        results[1].reshape(-1, widths[1]),
+        results[2].reshape(-1, widths[2]),
+        results[3].reshape(-1, down_in.shape[1]),
+        results[4],
+    ]
+
+
+class ReduceChunk:
+    def __init__(self, place, order, source, total, landings, sems, send_sems, recv_sems):
+        self.place, self.order, self.source = place, order, source
+        self.total, self.landings = total, landings
+        self.sem, self.send_sems, self.recv_sems = sems, send_sems, recv_sems
+        self.copies = {}
+
+    def region(self, stage, flipped):
+        full = self.order[stage:]
+        return self.place.region(full, (self.order[stage - 1],) if flipped else ())
+
+    def launch(self, stage):
+        core = self.place.bits[CORE]
+        if stage == 0:
+            local = pltpu.make_async_copy(self.source(core), self.total, self.sem)
+            local.start()
+            self.local = local
+            src, axis = self.source(1 - core), CORE
+        else:
+            axis = self.order[stage - 1]
+            src = self.total.at[self.region(stage, True)]
+        copy = send(
+            self.place, axis, src, self.landings[stage],
+            self.send_sems.at[stage], self.recv_sems.at[stage],
+        )
+        copy.start()
+        self.copies[stage] = copy
+
+    def absorb(self, stage):
+        self.copies[stage].wait_recv()
+        landing = self.landings[stage]
+        if stage == 0:
+            self.local.wait()
+            free = (0, 1, 2, 3)
+        else:
+            free = tuple(sorted(self.order[stage:]))
+        blocks = 2 ** len(free)
+
+        def add(block, carry):
+            index = list(self.place.bits[:CHIP_AXES])
+            where = []
+            rest = block
+            for axis in reversed(free):
+                bit = lax.rem(rest, 2)
+                rest = lax.div(rest, 2)
+                index[axis] = bit
+                where.insert(0, bit)
+            summed = self.total[tuple(index)].astype(jnp.float32) + landing[tuple(where)].astype(
+                jnp.float32
+            )
+            self.total[tuple(index)] = summed.astype(jnp.bfloat16)
+            return carry
+
+        lax.fori_loop(0, blocks, add, 0)
+
+    def last(self):
+        self.copies[CHIP_AXES].wait_recv()
+        return self.total[self.place.region((), ())].astype(jnp.float32) + self.landings[
+            CHIP_AXES
+        ][...].astype(jnp.float32)
+
+    def drain(self):
+        for copy in self.copies.values():
+            copy.wait_send()
+
+
+REDUCE_ORDERS = ((X, Y, ZN, ZF), (Y, X, ZN, ZF))
+
+
+def landing_shapes(rows, count):
+    return [
+        pltpu.VMEM((2,) * (CHIP_AXES - stage) + (rows, count), jnp.bfloat16)
+        for stage in range(CHIP_AXES + 1)
+    ]
+
+
+def reduce_plan(widths, down_shape):
+    plan = []
+    for tensor in (3, 2, 0, 1):
+        if tensor == 3:
+            half = down_shape[1] // 2
+            plan += [(3, 0, half, down_shape[0]), (3, half, half, down_shape[0])]
+        else:
+            half = widths[tensor] // 2
+            first = -(-half // 256) * 128
+            plan += [(tensor, 0, first, BLOCK), (tensor, first, half - first, BLOCK)]
+    return plan
+
+
+def reduce_kernel(widths, down_shape, *refs):
+    grads, small_in = refs[:4], refs[4]
+    outs, small_out = refs[5:9], refs[9]
+    refs = refs[10:]
+    plan = reduce_plan(widths, down_shape)
+    place = Place()
+    core = place.bits[CORE]
+    buffers = [refs[6 * k : 6 * k + 6] for k in range(len(plan))]
+    refs = refs[6 * len(plan) :]
+    (finals, refs) = (refs[:3], refs[3:])
+    small_values, small_landing, local_sems, final_send, final_recv, final_own = refs[:6]
+    small_send, small_recv, send_sems, recv_sems = refs[6:]
+    enter(place, range(5))
+    small_values[0] = small_in[...]
+
+    def small_copy(count):
+        return send(
+            place, count, small_values.at[count], small_landing.at[count],
+            small_send.at[count], small_recv.at[count],
+        )
+
+    chunks = []
+    for index, (tensor, start, count, rows) in enumerate(plan):
+        def source(bit, tensor=tensor, start=start, count=count, rows=rows):
+            every = (pl.ds(0, 2),) * CHIP_AXES
+            if tensor == 3:
+                return grads[3].at[every + (bit, pl.ds(0, rows), pl.ds(start, count))]
+            first = pl.multiple_of(bit * (widths[tensor] // 2) + start, 128)
+            return grads[tensor].at[every + (pl.ds(0, rows), pl.ds(first, count))]
+
+        chunks.append(
+            ReduceChunk(
+                place, REDUCE_ORDERS[index % 2], source, buffers[index][0], buffers[index][1:],
+                local_sems.at[index], send_sems.at[index], recv_sems.at[index],
+            )
+        )
+        chunks[-1].launch(0)
+    small_copy(0).start()
+    final_copies = []
+    pairs = len(chunks) // 2
+    for slot in range(pairs + 4):
+        if slot < 5:
+            small_copy(slot).wait()
+            small_values[slot + 1] = small_values[slot] + small_landing[slot]
+            if slot < 4:
+                small_copy(slot + 1).start()
+        for pair in range(pairs):
+            stage = slot - pair
+            for chunk in (2 * pair, 2 * pair + 1):
+                if 0 <= stage < CHIP_AXES:
+                    chunks[chunk].absorb(stage)
+                    chunks[chunk].launch(stage + 1)
+                elif stage == CHIP_AXES:
+                    tensor, start, count, rows = plan[chunk]
+                    if tensor == 3:
+                        outs[3][:, pl.ds(start, count)] = chunks[chunk].last()
+                    else:
+                        finals[tensor][:, pl.ds(start, count)] = chunks[chunk].last()
+            if stage == CHIP_AXES and plan[2 * pair][0] != 3:
+                tensor = plan[2 * pair][0]
+                half = widths[tensor] // 2
+                columns = pl.ds(pl.multiple_of(core * half, 128), half)
+                rows = BLOCK // 2
+                copy = send(
+                    place, CORE,
+                    finals[tensor].at[pl.ds(pl.multiple_of((1 - core) * rows, 8), rows)],
+                    outs[tensor].at[:, columns],
+                    final_send.at[tensor], final_recv.at[tensor],
+                )
+                copy.start()
+                final_copies.append(copy)
+                own = pltpu.make_async_copy(
+                    finals[tensor].at[pl.ds(pl.multiple_of(core * rows, 8), rows)],
+                    outs[tensor].at[:, columns],
+                    final_own.at[tensor],
+                )
+                own.start()
+                final_copies.append(own)
+    small_out[...] = small_values[5]
+    for copy in final_copies:
+        copy.wait()
+    for chunk in chunks:
+        chunk.drain()
+
+
+def reduce_grads(g_qkv, g_out, g_up, g_down, small_in, down_rows):
+    grid = (2, 2, 2, 2)
+    widths = (g_qkv.shape[1], g_out.shape[1], g_up.shape[1])
+    down_shape = (down_rows, g_down.shape[1])
+    grads = [
+        g.reshape(grid + (BLOCK, width)) for g, width in zip((g_qkv, g_out, g_up), widths)
+    ] + [g_down.reshape(grid + (2,) + down_shape)]
+    plan = reduce_plan(widths, down_shape)
+    scratch = []
+    for tensor, start, count, rows in plan:
+        scratch.append(pltpu.VMEM(grid + (rows, count), jnp.bfloat16))
+        scratch += landing_shapes(rows, count)
+    dma = pltpu.SemaphoreType.DMA
+    scratch += [pltpu.VMEM((BLOCK, width // 2), jnp.float32) for width in widths]
+    scratch += [
+        pltpu.VMEM((6,) + small_in.shape, jnp.float32),
+        pltpu.VMEM((5,) + small_in.shape, jnp.float32),
+        dma((len(plan),)),
+        dma((3,)),
+        dma((3,)),
+        dma((3,)),
+        dma((5,)),
+        dma((5,)),
+        dma((len(plan), 5)),
+        dma((len(plan), 5)),
+    ]
+    in_vmem = pl.BlockSpec(memory_space=pltpu.VMEM)
+    in_hbm = pl.BlockSpec(memory_space=pl.ANY)
+    outs = [jax.ShapeDtypeStruct((BLOCK // 2, width), jnp.float32) for width in widths] + [
+        jax.ShapeDtypeStruct(down_shape, jnp.float32),
+        jax.ShapeDtypeStruct(small_in.shape, jnp.float32),
+    ]
+    return pl.pallas_call(
+        partial(reduce_kernel, widths, down_shape),
+        out_shape=outs,
+        in_specs=[in_hbm] * 4 + [in_vmem],
+        out_specs=[in_vmem] * 5,
+        scratch_shapes=scratch,
+        compiler_params=pltpu.CompilerParams(
+            collective_id=2, has_side_effects=True, vmem_limit_bytes=56 * 2**20
+        ),
+        name="reduce_grads",
+    )(*grads, small_in)
+
+
+def device_index():
+    return lax.axis_index("wide") * lax.axis_size("narrow") + lax.axis_index("narrow")
+
+
+def spread(shard, whole):
+    row = jnp.zeros((whole,), jnp.float32)
+    return lax.dynamic_update_slice(
+        row, shard.astype(jnp.float32), (device_index() * shard.shape[0],)
+    )
+
+
+def pad_columns(values):
+    return jnp.pad(values, ((0, 0), (0, D - values.shape[1])))
+
+
+def gather_by_kernel(shards):
+    qkv, out, up, down, qv_bias, up_bias, gain_attn, gain_mlp = shards
+    devices = lax.axis_size("wide") * lax.axis_size("narrow")
+    small = jnp.concatenate(
+        [spread(v, v.shape[0] * devices) for v in (gain_attn, gain_mlp, qv_bias, up_bias)]
+    ).reshape(-1, D)
+    qkv_w, out_w, up_w, down_w, small = gather_weights(
+        qkv.astype(jnp.float32),
+        pad_columns(out).astype(jnp.float32),
+        up.astype(jnp.float32),
+        pad_columns(down),
+        small,
+    )
+    small = small.reshape(-1)
+    width = out.shape[1]
+    return (
+        qkv_w, out_w[:, :width], up_w, down_w[:, :width],
+        small[2 * D : 4 * D].astype(jnp.bfloat16), small[4 * D :].astype(jnp.bfloat16),
+        small[:D].astype(jnp.bfloat16), small[D : 2 * D].astype(jnp.bfloat16),
+    )
+
+
+def reduce_by_kernel(sums, grad_b_out, grad_b_down, down_rows):
+    w_qkv, w_out, b_qv, g_attn, w_up, w_down, b_up, g_mlp = sums
+    width = w_out.shape[1]
+    small = jnp.concatenate(
+        [g_attn, g_mlp, b_qv, b_up]
+        + [jnp.pad(v, (0, D - width)) for v in (grad_b_out, grad_b_down)]
+    ).reshape(-1, D)
+    rows = small.shape[0]
+    small = jnp.pad(small, ((0, -rows % 8), (0, 0)))
+    qkv, out, up, down, small = reduce_grads(
+        w_qkv.astype(jnp.bfloat16),
+        pad_columns(w_out).astype(jnp.bfloat16),
+        w_up.astype(jnp.bfloat16),
+        pad_columns(w_down).astype(jnp.bfloat16),
+        small,
+        down_rows,
+    )
+    small = small.reshape(-1)
+    devices = lax.axis_size("wide") * lax.axis_size("narrow")
+
+    def shard(first, count):
+        part = count // devices
+        return lax.dynamic_slice(small, (first + device_index() * part,), (part,))
+
+    every_shard = (
+        qkv, out[:, :width], shard(2 * D, 2 * D), shard(0, D), up, down[:, :width],
+        shard(4 * D, b_up.shape[0]), shard(D, D),
+    )
+    first = 4 * D + b_up.shape[0]
+    return every_shard, (small[first : first + width], small[first + D : first + D + width])
+
+
 def on_device(
+    by_kernel,
     resid,
     gain_attn,
     qkv_weight,
@@ -160,16 +719,12 @@
     seq_lengths,
 ):
     shards = (qkv_weight, out_weight, up_weight, down_weight, qv_bias, up_bias, gain_attn, gain_mlp)
-    gathered = (
-        lax.all_gather(shards[0], ("wide", "narrow"), axis=0, tiled=True),
-        lax.all_gather(shards[1], ("wide", "narrow"), axis=0, tiled=True),
-        lax.all_gather(shards[2], ("wide", "narrow"), axis=0, tiled=True),
-        lax.all_gather(shards[3], ("wide", "narrow"), axis=0, tiled=True),
-        lax.all_gather(shards[4], ("wide", "narrow"), axis=0, tiled=True),
-        lax.all_gather(shards[5], ("wide", "narrow"), axis=0, tiled=True),
-        lax.all_gather(shards[6], ("wide", "narrow"), axis=0, tiled=True),
-        lax.all_gather(shards[7], ("wide", "narrow"), axis=0, tiled=True),
-    )
+    if by_kernel:
+        gathered = gather_by_kernel(shards)
+    else:
+        gathered = tuple(
+            lax.all_gather(shard, ("wide", "narrow"), axis=0, tiled=True) for shard in shards
+        )
     row_count = resid.shape[0]
     places, segment = segment_ids(seq_lengths[0], row_count)
     resid_f = resid.astype(jnp.float32)
@@ -185,16 +740,7 @@
         + jnp.dot(mlp_first[2], gathered[3], preferred_element_type=jnp.float32)
         + down_bias.astype(jnp.float32)
     ).astype(jnp.bfloat16)
-    weights_back = (
-        lax.all_gather(shards[0], ("wide", "narrow"), axis=0, tiled=True),
-        lax.all_gather(shards[1], ("wide", "narrow"), axis=0, tiled=True),
-        lax.all_gather(shards[2], ("wide", "narrow"), axis=0, tiled=True),
-        lax.all_gather(shards[3], ("wide", "narrow"), axis=0, tiled=True),
-        lax.all_gather(shards[4], ("wide", "narrow"), axis=0, tiled=True),
-        lax.all_gather(shards[5], ("wide", "narrow"), axis=0, tiled=True),
-        lax.all_gather(shards[6], ("wide", "narrow"), axis=0, tiled=True),
-        lax.all_gather(shards[7], ("wide", "narrow"), axis=0, tiled=True),
-    )
+    weights_back = gathered
     normed_mlp, pre_act, activated = mlp_part(middle, weights_back)
     grad_out = cotangent.astype(jnp.float32)
     grad_w_down = contract_rows(activated, cotangent)
@@ -235,19 +781,19 @@
     first_value, first_pull = jax.vjp(compressed_norm, resid_f, weights_back[6].astype(jnp.float32))
     grad_resid_norm, grad_g_attn = first_pull(grad_normed)
     grad_resid = (grad_middle + grad_resid_norm).astype(jnp.bfloat16)
-    every_shard = (
-        lax.psum_scatter(grad_w_qkv, ("wide", "narrow"), scatter_dimension=0, tiled=True),
-        lax.psum_scatter(grad_w_out, ("wide", "narrow"), scatter_dimension=0, tiled=True),
-        lax.psum_scatter(grad_b_qv, ("wide", "narrow"), scatter_dimension=0, tiled=True),
-        lax.psum_scatter(grad_g_attn, ("wide", "narrow"), scatter_dimension=0, tiled=True),
-        lax.psum_scatter(grad_w_up, ("wide", "narrow"), scatter_dimension=0, tiled=True),
-        lax.psum_scatter(grad_w_down, ("wide", "narrow"), scatter_dimension=0, tiled=True),
-        lax.psum_scatter(grad_b_up, ("wide", "narrow"), scatter_dimension=0, tiled=True),
-        lax.psum_scatter(grad_g_mlp, ("wide", "narrow"), scatter_dimension=0, tiled=True),
-    )
+    sums = (
+        grad_w_qkv, grad_w_out, grad_b_qv, grad_g_attn, grad_w_up, grad_w_down, grad_b_up, grad_g_mlp
+    )
+    if by_kernel:
+        every_shard, bias_sums = reduce_by_kernel(sums, grad_b_out, grad_b_down, down_weight.shape[0])
+    else:
+        every_shard = tuple(
+            lax.psum_scatter(total, ("wide", "narrow"), scatter_dimension=0, tiled=True)
+            for total in sums
+        )
+        bias_sums = lax.psum((grad_b_out, grad_b_down), ("wide", "narrow"))
     attn_shards = every_shard[:4]
     mlp_shards = every_shard[4:]
-    bias_sums = lax.psum((grad_b_out, grad_b_down), ("wide", "narrow"))
     return (
         out_resid,
         grad_resid,
@@ -265,8 +811,9 @@
 
 
 def solution(mesh):
+    by_kernel = mesh.shape["wide"] == 8 and mesh.shape["narrow"] == 4
     return jax.shard_map(
-        on_device,
+        partial(on_device, by_kernel),
         mesh=mesh,
         in_specs=(
             P(("wide", "narrow"), None),

time: 836 us -> 479 us (0.57)
  waiting for transfers between devices: 444 us -> 0 us
  Pallas kernels: 0 us -> 176 us
  blocking collectives: 84.5 us -> 0 us
  matrix products: 197 us -> 177 us
  local copies, waits for them, and re-layouts: 36.7 us -> 56.1 us
  between operations: 15.2 us -> 1.95 us
    reduce_scatter x4 -> x0, waiting for transfers between devices: 333 us -> none  [the longest x1 142 us: on_device(): lax.psum_scatter(grad_w_up, ('wide', 'narrow'), scatter_dimension=0, tile...]
    pallas_call x0 -> x2, Pallas kernels: none -> 176 us  [the longest x1 90.5 us: gather_weights(): pl.pallas_call(gather_kernel, out_shape=outs, in_specs=[in_vmem] * 5, out...]
    all_gather x4 -> x0, waiting for transfers between devices: 108 us -> none  [the longest x1 54.3 us: on_device(): lax.all_gather(shards[3], ('wide', 'narrow'), axis=0, tiled=True)]
    unnamed x2 -> x0, blocking collectives: 84.5 us -> none
    dot_general x4, matrix products: 33.7 us -> 25 us  [contract_rows(): lax.dot_general(left_side, right_side, (((0,), (0,)), ((), ())), preferre...]
    unnamed x134 -> x130, local copies, waits for them, and re-layouts: 22 us -> 28 us
  transfers between devices with their start and end apart: 8 -> 0, of which waited for: 6 -> 0; matrix products, arithmetic and copies ran while one was open for 27% -> 0% of each run, Pallas kernels for 0% -> 0%
where the time goes in v1:
time: 479 us; the launch traced here: 471 us
  matrix products  177 us (37%)
  Pallas kernels  176 us (37%)
  other arithmetic  60.6 us (13%)
  local copies, waits for them, and re-layouts  56.1 us (12%)
    pallas_call x1, Pallas kernels, gather_weights(): pl.pallas_call(gather_kernel, out_shape=outs, in_specs=[in_vmem] * 5, out...  90.5 us
    pallas_call x1, Pallas kernels, reduce_grads(): pl.pallas_call(partial(reduce_kernel, widths, down_shape), out_shape=outs...  85.1 us
    dot_general x4, matrix products, contract_cols(): lax.dot_general(left_side, right_side, (((1,), (1,)), ((), ())), preferre...  31.9 us
    dot_general x2, matrix products, attend_backward(): jnp.einsum('qhd,khd->hqk', grad_block, value_heads[:last_row], preferred_...  28.1 us
    unnamed x130, local copies, waits for them, and re-layouts  28 us
    dot_general x4, matrix products, contract_rows(): lax.dot_general(left_side, right_side, (((0,), (0,)), ((), ())), preferre...  25 us
    convert_element_type x2, other arithmetic, attend_backward(): grad_scores = (attn_probs * (grad_probs - row_dot)).astype(jnp.bfloat16)  24.5 us
    dot_general x2, matrix products, attend_backward(): jnp.einsum('hqk,qhd->khd', attn_probs.astype(jnp.bfloat16), grad_block, p...  17.8 us

profile of v1, /device:TPU:0, one launch (start us, length us, event | category | flops | bytes accessed | tf_op | source)
XLA Modules:
  0.0 470.9 jit_solution(10379354843430033891)
XLA Ops:
  6.8 0.9 pad.42.down_in
  7.8 0.9 convert_element_type.160.qkv_in
  8.7 1.0 compare_and_fusion
  9.7 0.9 convert_element_type.162.up_in
  10.6 1.5 fusion.34
  12.0 1.7 copy.61
  14.1 2.6 copy.70
  17.3 1.3 copy-done.7
  18.7 90.5 %gather_weights.1 = (bf16[2,2,2,2,48,2304]{5,4,3,2,1,0:T(8,128)(2,1)S(1)}, bf16[2,2,2,2,48,768]{5,4,3,2,1,0:T(8,128)(2,1)S(1)}, bf16[2,2,2,2,48,3072]{5,4,3,2,1,...) custom-call(f32[24,2304]{1,0:T(8,128)S(1)} %convert_element_type.160.qkv_in, ...), custom_call_target="tpu_custom_call" | custom-call | tf_op jit(solution)/shard_map/gather_weights/pallas_call | solution.py:385
  109.2 1.8 copy-done
  111.2 7.0 %add_convert_fusion = bf16[1024,2304]{1,0:T(8,128)(2,1)S(1)} fusion(bf16[768,2304]{1,0:T(8,128)(2,1)} %bitcast.93, f32[2304]{0:T(1024)S(1)} %pad_maximum_fusion.6, f32[768]{0:T(1024)S(1)} %get-tuple-element.137, f32[1024]{0:T(1024)S(1)} %fusion.51, f32[1024,1]{0,1:T(1,128)S(1)} %bitcast.146, f32[1024,767]{0,1:T(8,128)} %copy-done.7), kind=kOutput, calls=%fused_computation.36 | convolution fusion | flops 3631742976 | bytes 11419648 | tf_op jit(solution)/shard_map/dot_general | solution.py:129
  118.2 1.7 fusion.66
  119.9 1.9 fusion.67
  121.7 2.6 copy.68
  124.3 2.3 copy.64
  126.6 2.3 copy.67
  129.0 2.3 copy.63
  131.3 2.3 copy.62
  133.6 3.0 copy.66
  136.6 3.4 fusion.23
  140.1 2.6 fusion.16
  142.7 1.3 log_add_fusion.1
  144.7 5.7 %fusion.48 = bf16[512,12,64]{0,2,1:T(8,128)(2,1)} fusion(bf16[512,12,64]{0,2,1:T(8,128)(2,1)} %bitcast.125, f32[12,512]{1,0:T(8,128)S(1)} %fusion.16, f32[12,512]{1,0:T(8,128)S(1)} %get-tuple-element.160, f32[12,512,512]{1,2,0:T(8,128)S(1)} %get-tuple-element.161, pred[512,512]{0,1:T(8,128)(4,1)} %compare_and_fusion), kind=kOutput, calls=%fused_computation.92 | convolution fusion | flops 418775040 | bytes 14467072 | tf_op jit(solution)/shard_map/hqk,khd->qhd/dot_general | solution.py:71
  150.4 10.7 %fusion.18 = (f32[12,512]{1,0:T(8,128)S(1)}, f32[12,512,1024]{2,1,0:T(8,128)}) fusion(pred[512,1024]{1,0:T(8,128)(4,1)S(1)} %copy-done.14, bf16[512,12,64]{0,2,1:T(8,128)(2,1)S(1)} %bitcast.106, bf16[1024,12,64]{0,2,1:T(8,128)(2,1)S(1)} %bitcast.102), kind=kOutput, calls=%fused_computation.37 | convolution fusion | flops 824174592 | bytes 28073984 | tf_op jit(solution)/shard_map/qhd,khd->hqk/dot_general | solution.py:46
  161.0 12.3 %fusion = f32[12,512]{1,0:T(8,128)S(1)} fusion(f32[12,512]{1,0:T(8,128)S(1)} %get-tuple-element.158, f32[12,512,1024]{2,1,0:T(8,128)} %get-tuple-element.159, pred[512,1024]{1,0:T(8,128)(4,1)S(1)} %copy-done.14), kind=kLoop, calls=%fused_computation.6 | loop fusion | flops 25159680 | bytes 25739264 | tf_op jit(solution)/shard_map/reduce_sum | solution.py:68
  174.0 2.5 copy-done.2
  176.4 8.6 %fusion.47 = bf16[512,12,64]{0,2,1:T(8,128)(2,1)} fusion(bf16[1024,12,64]{0,2,1:T(8,128)(2,1)S(1)} %bitcast.114, f32[12,512]{1,0:T(8,128)S(1)} %fusion, f32[12,512]{1,0:T(8,128)S(1)} %get-tuple-element.158, f32[12,512,1024]{2,1,0:T(8,128)S(1)} %copy-done.2, pred[512,1024]{1,0:T(8,128)(4,1)S(1)} %copy-done.14), kind=kOutput, calls=%fused_computation.91 | convolution fusion | flops 837156864 | bytes 28098560 | tf_op jit(solution)/shard_map/hqk,khd->qhd/dot_general | solution.py:71
  185.1 1.6 pad_maximum_fusion.3
  186.7 1.7 fusion.72
  188.7 0.9 slice-done.6
  190.1 8.4 %fusion.64 = f32[1024,3072]{1,0:T(8,128)} fusion(bf16[768,3072]{1,0:T(8,128)(2,1)S(1)} %bitcast.123, f32[768]{0:T(1024)S(1)} %get-tuple-element.136, f32[1024]{0:T(1024)S(1)} %fusion.52, f32[1024,1]{0,1:T(1,128)S(1)} %bitcast.139, f32[1024,767]{0,1:T(8,128)S(1)} %get-tuple-element.163), kind=kOutput, calls=%fused_computation.139 | convolution fusion | flops 4834983936 | bytes 20454400 | tf_op jit(solution)/shard_map/dot_general | solution.py:142
  198.6 10.6 %add_convert_fusion.1 = bf16[1024,767]{0,1:T(8,128)(2,1)} fusion(f32[1024,767]{0,1:T(8,128)S(1)} %get-tuple-element.163, bf16[3072,768]{1,0:T(8,128)(2,1)S(1)} %bitcast.155, f32[767]{0:T(1024)S(1)} %convert_element_type.179, f32[1024,3072]{1,0:T(8,128)} %fusion.64, f32[3072]{0:T(1024)S(1)} %reshape.459), kind=kOutput, calls=%fused_computation.69 | convolution fusion | flops 4859360256 | bytes 22029308 | tf_op jit(solution)/shard_map/dot_general | solution.py:740
  209.2 2.6 copy.74
  211.8 16.6 %convert_reduce_fusion = (f32[3072]{0:T(1024)}, bf16[1024,3072]{1,0:T(8,128)(2,1)S(1)}) fusion(f32[1024,3072]{1,0:T(8,128)} %fusion.64, f32[3072]{0:T(1024)S(1)} %reshape.459, bf16[1024,767]{1,0:T(8,128)(2,1)S(1)} %copy-done.29, bf16[3072,768]{1,0:T(8,128)(2,1)} %bitcast.152), kind=kOutput, calls=%fused_computation.23 | convolution fusion | flops 4897895424 | bytes 25188352 | tf_op jit(solution)/shard_map/dot_general | solution.py:33
  228.4 10.9 %convolution_convert_fusion = bf16[3072,767]{1,0:T(8,128)(2,1)S(1)} fusion(bf16[1024,767]{1,0:T(8,128)(2,1)S(1)} %copy-done.29, f32[1024,3072]{1,0:T(8,128)} %fusion.64, f32[3072]{0:T(1024)S(1)} %reshape.459), kind=kOutput, calls=%fused_computation.41 | convolution fusion | flops 4859360256 | bytes 18878464 | tf_op jit(solution)/shard_map/dot_general | solution.py:27
  239.3 8.4 %multiply_reduce_fusion.2 = (f32[768]{0:T(1024)S(1)}, f32[1024]{0:T(1024)S(1)}, f32[1024,768]{0,1:T(8,128)S(1)}) fusion(f32[1024]{0:T(1024)S(1)} %fusion.52, f32[1024,1]{0,1:T(1,128)S(1)} %bitcast.140, f32[1024,767]{0,1:T(8,128)S(1)} %copy-done.10, f32[768]{0:T(1024)S(1)} %get-tuple-element.136, bf16[1024,3072]{1,0:T(8,128)(2,1)S(1)} %get-tuple-element.171, ...), kind=kOutput, calls=%fused_computation.65 | convolution fusion | flops 4837341184 | bytes 17315840 | tf_op jit(solution)/shard_map/dot_general | solution.py:33
  248.4 6.9 %convolution_convert_fusion.1 = bf16[768,3072]{1,0:T(8,128)(2,1)} fusion(bf16[1024,3072]{1,0:T(8,128)(2,1)S(1)} %get-tuple-element.171, f32[768]{0:T(1024)S(1)} %get-tuple-element.136, f32[1024]{0:T(1024)S(1)} %fusion.52, f32[1024,1]{0,1:T(1,128)S(1)} %bitcast.142, f32[1024,767]{0,1:T(8,128)S(1)} %copy-done.10), kind=kOutput, calls=%fused_computation.42 | convolution fusion | flops 4837343232 | bytes 14162944 | tf_op jit(solution)/shard_map/dot_general | solution.py:27
  255.4 2.6 pad.44
  259.4 1.4 convolution_convert_fusion.4
  260.8 1.2 pad.43
  262.0 1.4 convolution_convert_fusion.3
  263.4 1.0 fusion.68
  264.4 0.9 copy-done.28
  265.4 4.0 fusion.40
  269.4 13.8 %fusion.32 = bf16[1024,12,64]{0,2,1:T(8,128)(2,1)} fusion(f32[512,12,64]{0,2,1:T(8,128)} %fusion.40, bf16[512,12,64]{0,2,1:T(8,128)(2,1)} %bitcast.129, f32[12,512]{1,0:T(8,128)S(1)} %copy-done.33, f32[12,512,1024]{2,1,0:T(8,128)} %get-tuple-element.159, pred[512,1024]{1,0:T(8,128)(4,1)} %fusion.34), kind=kOutput, calls=%fused_computation.61 | convolution fusion | flops 832045056 | bytes 29646848 | tf_op jit(solution)/shard_map/hqk,qhd->khd/dot_general | solution.py:114
  283.2 9.8 %multiply_reduce_fusion.1 = (f32[12,512]{1,0:T(8,128)S(1)}, f32[12,512,512]{1,2,0:T(8,128)}) fusion(f32[12,512]{1,0:T(8,128)S(1)} %copy-done.36, f32[12,512,512]{1,2,0:T(8,128)S(1)} %bitcast.100, pred[512,512]{0,1:T(8,128)(4,1)S(1)} %copy-done.23, bf16[512,12,64]{0,2,1:T(8,128)(2,1)} %bitcast.128, bf16[512,12,64]{0,2,1:T(8,128)(2,1)} %bitcast.126), kind=kOutput, calls=%fused_computation.26 | convolution fusion | flops 418375680 | bytes 27049984 | tf_op jit(solution)/shard_map/qhd,khd->hqk/dot_general | solution.py:95
  293.1 7.0 %multiply_convert_fusion.1 = bf16[12,512,512]{1,2,0:T(8,128)(2,1)S(1)} fusion(f32[12,512,512]{1,2,0:T(8,128)} %get-tuple-element.166, f32[12,512]{1,0:T(8,128)S(1)} %get-tuple-element.165, f32[12,512]{1,0:T(8,128)S(1)} %copy-done.36, f32[12,512,512]{1,2,0:T(8,128)S(1)} %bitcast.100, pred[512,512]{0,1:T(8,128)(4,1)S(1)} %copy-done.23), kind=kLoop, calls=%fused_computation.25 | loop fusion | flops 18874368 | bytes 31768576 | tf_op jit(solution)/shard_map/convert_element_type | solution.py:99
  300.1 2.0 fusion.46
  302.1 3.2 multiply_bitcast_fusion
  305.3 18.3 %multiply_reduce_fusion = (f32[12,512]{1,0:T(8,128)S(1)}, f32[12,512,1024]{2,1,0:T(8,128)}) fusion(f32[12,512]{1,0:T(8,128)S(1)} %copy-done.33, f32[12,512,1024]{2,1,0:T(8,128)} %get-tuple-element.159, pred[512,1024]{1,0:T(8,128)(4,1)S(1)} %copy-done.15, bf16[512,12,64]{0,2,1:T(8,128)(2,1)} %bitcast.130, bf16[1024,12,64]{0,2,1:T(8,128)(2,1)} %bitcast.113), kind=kOutput, calls=%fused_computation.1 | convolution fusion | flops 836757504 | bytes 53264384 | tf_op jit(solution)/shard_map/qhd,khd->hqk/dot_general | solution.py:95
  323.6 17.5 %multiply_convert_fusion = bf16[12,512,1024]{2,1,0:T(8,128)(2,1)S(1)} fusion(f32[12,512,1024]{2,1,0:T(8,128)} %get-tuple-element.168, f32[12,512]{1,0:T(8,128)S(1)} %get-tuple-element.167, f32[12,512]{1,0:T(8,128)S(1)} %copy-done.33, f32[12,512,1024]{2,1,0:T(8,128)} %get-tuple-element.159, pred[512,1024]{1,0:T(8,128)(4,1)S(1)} %copy-done.15), kind=kLoop, calls=%fused_computation | loop fusion | flops 37748736 | bytes 63488000 | tf_op jit(solution)/shard_map/convert_element_type | solution.py:99
  341.2 4.5 copy-done.4
  345.7 2.4 fusion.33
  348.2 10.0 %fusion.45 = bf16[512,12,64]{0,2,1:T(8,128)(2,1)} fusion(bf16[1024,12,64]{0,2,1:T(8,128)(2,1)S(1)} %bitcast.103, bf16[12,512,1024]{2,1,0:T(8,128)(2,1)} %copy-done.4), kind=kOutput, calls=%fused_computation.89 | convolution fusion | flops 806092800 | bytes 14942208 | tf_op jit(solution)/shard_map/hqk,khd->qhd/dot_general | solution.py:101
  358.1 1.3 pad_maximum_fusion.4
  359.5 5.5 %multiply_reduce_fusion.3 = (f32[768]{0:T(1024)S(1)}, f32[1024]{0:T(1024)S(1)}, f32[1024,768]{0,1:T(8,128)S(1)}) fusion(f32[1024]{0:T(1024)S(1)} %copy-done.46, f32[1024,1]{0,1:T(1,128)S(1)} %bitcast.147, f32[1024,767]{0,1:T(8,128)S(1)} %copy-done.8, f32[768]{0:T(1024)S(1)} %copy-done.44, bf16[768,2304]{1,0:T(8,128)(2,1)S(1)} %bitcast.94, ...), kind=kOutput, calls=%fused_computation.66 | convolution fusion | flops 3643537664 | bytes 14563328 | tf_op jit(solution)/shard_map/dot_general | solution.py:33
  365.8 1.2 copy-done.6
  367.0 1.9 convert_reduce_fusion.2
  369.4 1.0 convert_reduce_fusion.1
  370.4 5.7 %convolution_convert_fusion.2 = bf16[768,2304]{1,0:T(8,128)(2,1)} fusion(bf16[1024,768]{0,1:T(8,128)(2,1)S(1)} %bitcast.135, bf16[1024,768]{0,1:T(8,128)(2,1)S(1)} %bitcast.110, bf16[1024,768]{0,1:T(8,128)(2,1)S(1)} %bitcast.117, f32[768]{0:T(1024)S(1)} %copy-done.44, f32[1024]{0:T(1024)S(1)} %copy-done.46, f32[1024,1]{0,1:T(1,128)S(1)} %bitcast.149, ...), kind=kOutput, calls=%fused_computation.43 | convolution fusion | flops 3642949632 | bytes 11410432 | tf_op jit(solution)/shard_map/dot_general | solution.py:27
  376.8 85.1 %reduce_grads.1 = (f32[24,2304]{1,0:T(8,128)}, f32[24,768]{1,0:T(8,128)}, f32[24,3072]{1,0:T(8,128)}, f32[96,768]{1,0:T(8,128)}, f32[16,768]{1,0:T(8,128)}) custom-call(bf16[2,2,2,2,48,2304]{5,4,3,2,1,0:T(8,128)(2,1)} %bitcast.124, bf16[2,2,2,2,48,768]{5,4,3,2,1,0:T(8,128)(2,1)} %bitcast.118, bf16[2,2,2,2,48,3072]{5,4,3,2,1,0:T(8,128)(2,1)} %bitcast.119, ...), custom_call_target="tpu_custom_call" | custom-call | tf_op jit(solution)/shard_map/reduce_grads/pallas_call | solution.py:623
  462.0 0.9 reshape.456
  465.2 1.6 copy.75
  466.8 1.6 copy.97
  (174 shorter events, 17.7 us)
Async XLA Ops:
  14.0 97.1 %copy-start.38 = (f32[1024]{0:T(1024)}, f32[1024]{0:T(1024)S(1)}, u32[]{:S(2)}) copy-start(f32[1024]{0:T(1024)S(1)} %neg.38) | copy-start | bytes 12292
  17.0 1.6 copy-start.7
  18.7 92.4 %copy-start.40 = (f32[1024]{0:T(1024)}, f32[1024]{0:T(1024)S(1)}, u32[]{:S(2)}) copy-start(f32[1024]{0:T(1024)S(1)} %multiply_reduce_fusion.7) | copy-start | bytes 12292
  18.7 99.5 %copy-start.45 = (f32[1024]{0:T(1024)}, f32[1024]{0:T(1024)S(1)}, u32[]{:S(2)}) copy-start(f32[1024]{0:T(1024)S(1)} %fusion.51) | copy-start | bytes 12292
  109.2 1.8 copy-start
  111.1 7.1 %copy-start.43 = (f32[768]{0:T(1024)}, f32[768]{0:T(1024)S(1)}, u32[]{:S(2)}) copy-start(f32[768]{0:T(1024)S(1)} %get-tuple-element.137) | copy-start | bytes 9220
  129.0 7.7 %copy-start.22 = (pred[512,512]{0,1:T(8,128)(4,1)S(1)}, pred[512,512]{0,1:T(8,128)(4,1)}, u32[]{:S(2)}) copy-start(pred[512,512]{0,1:T(8,128)(4,1)} %compare_and_fusion) | copy-start | bytes 786436
  140.1 4.6 copy-start.3
  144.7 5.7 %copy-start.12 = (bf16[1024,768]{0,1:T(8,128)(2,1)S(1)}, bf16[1024,768]{0,1:T(8,128)(2,1)}, u32[]{:S(2)}) copy-start(bf16[1024,768]{0,1:T(8,128)(2,1)} %copy.68) | copy-start | bytes 4718596
  144.7 5.7 %copy-start.14 = (pred[512,1024]{1,0:T(8,128)(4,1)S(1)}, pred[512,1024]{1,0:T(8,128)(4,1)}, u32[]{:S(2)}) copy-start(pred[512,1024]{1,0:T(8,128)(4,1)} %fusion.34) | copy-start | bytes 1572868
  144.7 5.7 %copy-start.17 = (bf16[512,768]{0,1:T(8,128)(2,1)S(1)}, bf16[512,768]{0,1:T(8,128)(2,1)}, u32[]{:S(2)}) copy-start(bf16[512,768]{0,1:T(8,128)(2,1)} %copy.67) | copy-start | bytes 2359300
  150.3 23.6 %copy-start.25 = (bf16[1024,768]{0,1:T(8,128)(2,1)S(1)}, bf16[1024,768]{0,1:T(8,128)(2,1)}, u32[]{:S(2)}) copy-start(bf16[1024,768]{0,1:T(8,128)(2,1)} %copy.66) | copy-start | bytes 4718596
  161.0 15.4 %copy-start.2 = (f32[12,512,1024]{2,1,0:T(8,128)S(1)}, f32[12,512,1024]{2,1,0:T(8,128)}, u32[]{:S(2)}) copy-start(f32[12,512,1024]{2,1,0:T(8,128)} %get-tuple-element.159) | copy-start | bytes 75497472
  186.7 1.7 copy-start.30
  186.7 2.9 slice-start.6
  186.7 3.4 slice-start.7
  186.7 11.9 %slice-start.8 = ((s8[4718592]{0:T(1024)(128)(4,1)}), s8[524288]{0:T(1024)(128)(4,1)S(1)}, s32[]{:S(2)}) async-start(s8[4718592]{0:T(1024)(128)(4,1)} %bitcast.153), calls=%async_computation.8 | async-start | bytes 1048576
  188.4 10.1 %copy-start.9 = (f32[1024,767]{0,1:T(8,128)}, f32[1024,767]{0,1:T(8,128)S(1)}, u32[]{:S(2)}) copy-start(f32[1024,767]{0,1:T(8,128)S(1)} %get-tuple-element.163) | copy-start | bytes 9424900
  190.1 8.5 %slice-start.9 = ((s8[4718592]{0:T(1024)(128)(4,1)}), s8[4194304]{0:T(1024)(128)(4,1)S(1)}, s32[]{:S(2)}) async-start(s8[4718592]{0:T(1024)(128)(4,1)} %bitcast.153), calls=%async_computation.9 | async-start | bytes 8388608
  198.6 13.2 %copy-start.29 = (bf16[1024,767]{1,0:T(8,128)(2,1)S(1)}, bf16[1024,767]{1,0:T(8,128)(2,1)}, u32[]{:S(2)}) copy-start(bf16[1024,767]{1,0:T(8,128)(2,1)} %param.36) | copy-start | bytes 4712452
  228.4 10.9 %copy-start.10 = (f32[1024,767]{0,1:T(8,128)S(1)}, f32[1024,767]{0,1:T(8,128)}, u32[]{:S(2)}) copy-start(f32[1024,767]{0,1:T(8,128)} %copy-done.9) | copy-start | bytes 9424900
  248.4 9.6 %copy-start.5 = (f32[1024,768]{0,1:T(8,128)}, f32[1024,768]{0,1:T(8,128)S(1)}, u32[]{:S(2)}) copy-start(f32[1024,768]{0,1:T(8,128)S(1)} %add_add_fusion.1) | copy-start | bytes 9437188
  255.4 2.7 copy-start.11
  258.0 1.4 copy-start.31
  259.4 5.9 %slice-start = ((s8[12582912]{0:T(1024)(128)(4,1)}), s8[4194304]{0:T(1024)(128)(4,1)S(1)}, s32[]{:S(2)}) async-start(s8[12582912]{0:T(1024)(128)(4,1)} %bitcast.97), calls=%async_computation | async-start | bytes 8388608
  259.4 5.9 %slice-start.1 = ((s8[12582912]{0:T(1024)(128)(4,1)}), s8[4194304]{0:T(1024)(128)(4,1)S(1)}, s32[]{:S(2)}) async-start(s8[12582912]{0:T(1024)(128)(4,1)} %bitcast.97), calls=%async_computation.1 | async-start | bytes 8388608
  262.0 3.3 slice-start.2
  262.0 3.3 copy-start.23
  262.0 3.3 copy-start.36
  264.4 0.9 copy-start.28
  265.4 4.0 copy-start.33
  265.4 17.8 %slice-start.3 = ((s8[12582912]{0:T(1024)(128)(4,1)}), s8[4194304]{0:T(1024)(128)(4,1)S(1)}, s32[]{:S(2)}) async-start(s8[12582912]{0:T(1024)(128)(4,1)} %bitcast.99), calls=%async_computation.3 | async-start | bytes 8388608
  269.4 13.8 %slice-start.4 = ((s8[12582912]{0:T(1024)(128)(4,1)}), s8[4194304]{0:T(1024)(128)(4,1)S(1)}, s32[]{:S(2)}) async-start(s8[12582912]{0:T(1024)(128)(4,1)} %bitcast.99), calls=%async_computation.4 | async-start | bytes 8388608
  269.4 13.9 %slice-start.5 = ((s8[12582912]{0:T(1024)(128)(4,1)}), s8[4194304]{0:T(1024)(128)(4,1)S(1)}, s32[]{:S(2)}) async-start(s8[12582912]{0:T(1024)(128)(4,1)} %bitcast.99), calls=%async_computation.5 | async-start | bytes 8388608
  293.1 7.0 %copy-start.16 = (bf16[512,768]{0,1:T(8,128)(2,1)S(1)}, bf16[512,768]{0,1:T(8,128)(2,1)}, u32[]{:S(2)}) copy-start(bf16[512,768]{0,1:T(8,128)(2,1)} %copy.64) | copy-start | bytes 2359300
  300.1 2.0 copy-start.21
  302.1 3.2 copy-start.15
  323.6 22.1 %copy-start.18 = (bf16[512,768]{0,1:T(8,128)(2,1)S(1)}, bf16[512,768]{0,1:T(8,128)(2,1)}, u32[]{:S(2)}) copy-start(bf16[512,768]{0,1:T(8,128)(2,1)} %copy.67) | copy-start | bytes 2359300
  323.6 22.1 %copy-start.27 = (f32[512,12,64]{0,2,1:T(8,128)S(1)}, f32[512,12,64]{0,2,1:T(8,128)}, u32[]{:S(2)}) copy-start(f32[512,12,64]{0,2,1:T(8,128)} %multiply_bitcast_fusion) | copy-start | bytes 4718596
  341.1 4.5 copy-start.4
  345.7 2.4 copy-start.13
  348.1 11.4 %copy-start.19 = (bf16[1024,12,64]{0,2,1:T(8,128)(2,1)}, bf16[1024,12,64]{0,2,1:T(8,128)(2,1)S(1)}, u32[]{:S(2)}) copy-start(bf16[1024,12,64]{0,2,1:T(8,128)(2,1)S(1)} %fusion.33) | copy-start | bytes 4718596
  348.1 10.1 %copy-start.24 = (bf16[512,12,64]{0,2,1:T(8,128)(2,1)S(1)}, bf16[512,12,64]{0,2,1:T(8,128)(2,1)}, u32[]{:S(2)}) copy-start(bf16[512,12,64]{0,2,1:T(8,128)(2,1)} %fusion.46) | copy-start | bytes 2359300
  348.1 11.4 %copy-start.1 = (bf16[2,2,2,2,48,2304]{5,4,3,2,1,0:T(8,128)(2,1)S(1)}, bf16[2,2,2,2,48,2304]{5,4,3,2,1,0:T(8,128)(2,1)}, u32[]{:S(2)}) copy-start(bf16[2,2,2,2,48,2304]{5,4,3,2,1,0:T(8,128)(2,1)} %copy-done) | copy-start | bytes 10616836
  348.1 11.4 %copy-start.8 = (f32[1024,767]{0,1:T(8,128)S(1)}, f32[1024,767]{0,1:T(8,128)}, u32[]{:S(2)}) copy-start(f32[1024,767]{0,1:T(8,128)} %copy-done.7) | copy-start | bytes 9424900
  348.1 11.4 %copy-start.39 = (f32[1024]{0:T(1024)S(1)}, f32[1024]{0:T(1024)}, u32[]{:S(2)}) copy-start(f32[1024]{0:T(1024)} %copy-done.38) | copy-start | bytes 12292
  348.1 11.4 %copy-start.44 = (f32[768]{0:T(1024)S(1)}, f32[768]{0:T(1024)}, u32[]{:S(2)}) copy-start(f32[768]{0:T(1024)} %copy-done.43) | copy-start | bytes 9220
  348.1 11.4 %copy-start.46 = (f32[1024]{0:T(1024)S(1)}, f32[1024]{0:T(1024)}, u32[]{:S(2)}) copy-start(f32[1024]{0:T(1024)} %copy-done.45) | copy-start | bytes 12292
  359.5 5.6 %copy-start.42 = (f32[7680]{0:T(1024)S(1)}, f32[7680]{0:T(1024)}, u32[]{:S(2)}) copy-start(f32[7680]{0:T(1024)} %custom-call) | copy-start | bytes 92164
  359.5 5.6 %copy-start.41 = (f32[1024]{0:T(1024)S(1)}, f32[1024]{0:T(1024)}, u32[]{:S(2)}) copy-start(f32[1024]{0:T(1024)} %copy-done.40) | copy-start | bytes 12292
  365.2 1.9 copy-start.6
  367.0 1.9 copy-start.20
  367.0 2.4 copy-start.32
  370.4 5.7 %copy-start.47 = (f32[3072]{0:T(1024)S(1)}, f32[3072]{0:T(1024)}, u32[]{:S(2)}) copy-start(f32[3072]{0:T(1024)} %get-tuple-element.170) | copy-start | bytes 36868
  376.8 88.4 %copy-start.26 = (bf16[1024,767]{0,1:T(8,128)(2,1)S(1)}, bf16[1024,767]{0,1:T(8,128)(2,1)}, u32[]{:S(2)}) copy-start(bf16[1024,767]{0,1:T(8,128)(2,1)} %get-tuple-element.149) | copy-start | bytes 4712452
  462.0 6.5 %copy-start.37 = (f32[24,768]{1,0:T(8,128)S(1)}, f32[24,768]{1,0:T(8,128)}, u32[]{:S(2)}) copy-start(f32[24,768]{1,0:T(8,128)} %get-tuple-element.93) | copy-start | bytes 221188
  462.0 7.1 %copy-start.35 = (f32[24,3072]{1,0:T(8,128)S(1)}, f32[24,3072]{1,0:T(8,128)}, u32[]{:S(2)}) copy-start(f32[24,3072]{1,0:T(8,128)} %get-tuple-element.192) | copy-start | bytes 884740
  462.0 7.8 %copy-start.34 = (f32[96,768]{1,0:T(8,128)S(1)}, f32[96,768]{1,0:T(8,128)}, u32[]{:S(2)}) copy-start(f32[96,768]{1,0:T(8,128)} %get-tuple-element.95) | copy-start | bytes 884740

commit v2 on v0

--- a/solution.py
+++ b/solution.py
@@ -3,15 +3,1050 @@
 import jax
 import jax.numpy as jnp
 from jax import lax
+from jax.experimental import pallas as pl
+from jax.experimental.pallas import tpu as pltpu
 from jax.sharding import PartitionSpec as P
 
 D = 768
 H = 12
 HD = 64
-
+LANES = 128
+ROWS = 256
+FF_BLOCK = 768
+GROUP = 256
+GROUPS = D // GROUP
+TICKS = 2
 
 norm_eps = 1e-05
 masked_score = -1e30
+gelu_root = 0.7978845608028654
+
+bf16 = jnp.bfloat16
+f32 = jnp.float32
+
+MESH = pl.DeviceIdType.MESH
+ZF, ZN, Y, X, CORE = range(5)
+CHIP_AXES = 4
+BLOCK = 48
+
+
+NN = (((1,), (0,)), ((), ()))
+NT = (((1,), (1,)), ((), ()))
+TN = (((0,), (0,)), ((), ()))
+
+
+def dot(left, right, dims=NN):
+    return lax.dot_general(left, right, dims, preferred_element_type=f32)
+
+
+def column_sum(values):
+    return jnp.sum(values, axis=0, keepdims=True)
+
+
+def aligned(index, multiple):
+    return pl.multiple_of(index, multiple)
+
+
+class Place:
+    def __init__(self):
+        wide = lax.axis_index("wide")
+        narrow = lax.axis_index("narrow")
+        self.wide, self.narrow = wide, narrow
+        self.bits = (
+            lax.div(wide, 4),
+            lax.rem(lax.div(wide, 2), 2),
+            lax.rem(wide, 2),
+            lax.div(narrow, 2),
+            lax.rem(narrow, 2),
+        )
+        self.core = self.bits[CORE]
+
+    def other(self, axis):
+        flip = 1 - 2 * self.bits[axis]
+        if axis == X:
+            return (self.wide, self.narrow + 2 * flip)
+        if axis == CORE:
+            return (self.wide, self.narrow + flip)
+        return (self.wide + (4, 2, 1)[axis] * flip, self.narrow)
+
+    def region(self, full=(), flipped=()):
+        return tuple(
+            pl.ds(0, 2)
+            if axis in full
+            else (1 - self.bits[axis] if axis in flipped else self.bits[axis])
+            for axis in range(CHIP_AXES)
+        )
+
+
+def enter(place):
+    barrier = pltpu.get_barrier_semaphore()
+    for axis in range(5):
+        pl.semaphore_signal(
+            barrier, inc=1, device_id=place.other(axis), device_id_type=MESH
+        )
+    pl.semaphore_wait(barrier, 5)
+
+
+def send(place, axis, src, dst, send_sem, recv_sem):
+    return pltpu.make_async_remote_copy(
+        src_ref=src,
+        dst_ref=dst,
+        send_sem=send_sem,
+        recv_sem=recv_sem,
+        device_id=place.other(axis),
+        device_id_type=MESH,
+    )
+
+
+GATHER_COPIES = 15
+
+
+class GatherChunk:
+    def __init__(self, place, order, view, send_sems, recv_sems):
+        self.place, self.axes, self.view = place, order + (CORE,), view
+        self.send_sems, self.recv_sems = send_sems, recv_sems
+
+    def copy(self, stage, piece, arriving=False):
+        axis = self.axes[stage - 1]
+        flipped = (self.axes[piece - 1],) if piece else ()
+        bit = self.place.core
+        if arriving and axis == CORE:
+            bit = 1 - bit
+        elif arriving:
+            flipped += (axis,)
+        where = self.view(self.place.region(self.axes[: max(piece - 1, 0)], flipped), bit)
+        slot = stage * (stage - 1) // 2 + piece
+        return send(
+            self.place, axis, where, where, self.send_sems.at[slot], self.recv_sems.at[slot]
+        )
+
+    def step(self, stage):
+        for piece in range(stage):
+            self.copy(stage, piece, arriving=True).wait_recv()
+        for later in range(stage + 1, CHIP_AXES + 2):
+            self.copy(later, stage).start()
+
+    def drain(self):
+        for stage in range(1, CHIP_AXES + 2):
+            for piece in range(stage):
+                self.copy(stage, piece).wait_send()
+
+
+class ReduceChunk:
+    def __init__(self, place, order, view, lead, landings, send_sems, recv_sems):
+        self.place, self.order, self.view, self.lead = place, order, view, lead
+        self.landings, self.send_sems, self.recv_sems = landings, send_sems, recv_sems
+
+    def copy(self, stage):
+        if stage == 0:
+            axis = CORE
+            src = self.view(self.place.region(range(CHIP_AXES)), 1 - self.place.core)
+        else:
+            axis = self.order[stage - 1]
+            src = self.view(
+                self.place.region(self.order[stage:], (axis,)), self.place.core
+            )
+        return send(
+            self.place, axis, src, self.landings[stage],
+            self.send_sems.at[stage], self.recv_sems.at[stage],
+        )
+
+    def launch(self, stage):
+        self.copy(stage).start()
+
+    def absorb(self, stage):
+        self.copy(stage).wait_recv()
+        landing = self.landings[stage]
+        free = tuple(sorted(self.order[stage:]))
+
+        def add(block, carry):
+            index = list(self.place.bits[:CHIP_AXES])
+            where = ()
+            rest = block
+            for axis in reversed(free):
+                index[axis] = lax.rem(rest, 2)
+                where = (index[axis],) + where
+                rest = lax.div(rest, 2)
+            here = self.view(tuple(index), self.place.core)
+            here[...] = here[...] + landing[self.lead + where]
+            return carry
+
+        lax.fori_loop(0, 2 ** len(free), add, 0)
+        self.launch(stage + 1)
+
+    def total(self):
+        self.copy(CHIP_AXES).wait_recv()
+        here = self.view(self.place.region(), self.place.core)
+        return here[...].astype(f32) + self.landings[CHIP_AXES][...].astype(f32)
+
+    def drain(self):
+        for stage in range(CHIP_AXES + 1):
+            self.copy(stage).wait_send()
+
+
+def weight_chunks(weights):
+    qkv_w, out_w, up_w, down_w = weights
+    block = pl.ds(0, BLOCK)
+
+    def qkv_view(group):
+        def view(region, bit):
+            columns = pl.ds(aligned(group * GROUP + bit * LANES, LANES), LANES)
+            return qkv_w.at[(pl.ds(0, 3),) + region + (block, columns)]
+
+        return view
+
+    def half_view(whole, start, count):
+        half = whole.shape[-1] // 2
+
+        def view(region, bit):
+            return whole.at[region + (block, pl.ds(aligned(bit * half + start, LANES), count))]
+
+        return view
+
+    def down_view(start, count):
+        def view(region, bit):
+            return down_w.at[region + (bit, pl.ds(0, down_w.shape[-2]), pl.ds(start, count))]
+
+        return view
+
+    half = up_w.shape[-1] // 4
+    third = down_w.shape[-1] // 2
+    return [
+        (qkv_view(0), (3,), (BLOCK, LANES)),
+        (qkv_view(1), (3,), (BLOCK, LANES)),
+        (qkv_view(2), (3,), (BLOCK, LANES)),
+        (half_view(out_w, 0, out_w.shape[-1] // 2), (), (BLOCK, out_w.shape[-1] // 2)),
+        (half_view(up_w, 0, half), (), (BLOCK, half)),
+        (half_view(up_w, half, half), (), (BLOCK, half)),
+        (down_view(0, third), (), (down_w.shape[-2], third)),
+        (down_view(third, third), (), (down_w.shape[-2], third)),
+    ]
+
+
+CHUNKS = 8
+Q0, Q1, Q2, OUT, UP_A, UP_B, DOWN_A, DOWN_B = range(CHUNKS)
+
+GATHER_ORDERS = {
+    Q0: (ZF, ZN, Y, X),
+    Q1: (ZF, ZN, X, Y),
+    Q2: (Y, X, ZF, ZN),
+    OUT: (X, Y, ZF, ZN),
+    UP_A: (ZF, ZN, Y, X),
+    UP_B: (ZF, ZN, X, Y),
+    DOWN_A: (ZF, ZN, Y, X),
+    DOWN_B: (ZF, ZN, X, Y),
+}
+REDUCE_ORDERS = {
+    Q0: (X, Y, ZN, ZF),
+    Q1: (Y, X, ZN, ZF),
+    Q2: (X, Y, ZN, ZF),
+    OUT: (Y, X, ZN, ZF),
+    UP_A: (X, Y, ZN, ZF),
+    UP_B: (Y, X, ZN, ZF),
+    DOWN_A: (X, Y, ZN, ZF),
+    DOWN_B: (Y, X, ZN, ZF),
+}
+
+GATHER_STEPS = {
+    "FIRST": [(Q0, 0), (Q1, 0), (Q2, 0), (Q0, 1), (Q2, 1), (Q1, 1), (UP_A, 0), (UP_B, 0), (Q2, 2), (Q0, 2), (OUT, 0), (Q1, 2), (Q0, 3), (UP_A, 1), (OUT, 1), (Q1, 3), (UP_B, 1), (OUT, 2), (Q0, 4), (Q2, 3), (Q0, 5)],
+    "FORWARD": [[(Q1, 4), (UP_A, 2), (DOWN_A, 0), (DOWN_B, 0)], [(Q1, 5), (UP_B, 2)], [], [(OUT, 3), (UP_A, 3)], [(Q2, 4)], [], [(Q2, 5), (UP_B, 3), (DOWN_A, 1)], [], [(DOWN_B, 1)], [(OUT, 4), (UP_A, 4)], [(UP_B, 4), (DOWN_A, 2)], [(OUT, 5), (UP_A, 5), (DOWN_B, 2)]],
+    "NORMED": [],
+    "UP": [(UP_B, 5)],
+    "FEED": [[], [(DOWN_A, 3)], [(DOWN_B, 3)], [], [], [], [], [], [], [], [(DOWN_A, 4)], [(DOWN_B, 4)]],
+    "BACK": [(DOWN_A, 5), (DOWN_B, 5)],
+}
+
+REDUCE_STEPS = {
+    "GRAD_UP": [[], [], [(DOWN_A, 0)], [(DOWN_B, 0)]],
+    "PREPARED": [(UP_A, 0), (UP_B, 0), (OUT, 0)],
+    "BACKWARD": [[], [], [(DOWN_A, 1)], [(DOWN_B, 1)], [], [(Q0, 0)], [(UP_A, 1), (UP_B, 1)], [], [], [(Q0, 1), (Q1, 0), (DOWN_B, 3)], [(DOWN_A, 2)], [(UP_B, 2)]],
+    "FINISHED": [[], [(DOWN_B, 2), (OUT, 1)], [(DOWN_A, 3), (UP_A, 2), (OUT, 2)]],
+    "NORM": [(UP_B, 3), (Q0, 2), (Q2, 0)],
+    "REST": [(UP_A, 3), (Q1, 1), (OUT, 3), (Q0, 3), (Q2, 1), (Q1, 2), (Q2, 2), (Q1, 3), (Q2, 3)],
+}
+
+
+class SmallSum:
+    def __init__(self, place, values, landing, send_sems, recv_sems):
+        self.place, self.values, self.landing = place, values, landing
+        self.send_sems, self.recv_sems = send_sems, recv_sems
+
+    def copy(self, axis):
+        return send(
+            self.place, axis, self.values.at[axis], self.landing.at[axis],
+            self.send_sems.at[axis], self.recv_sems.at[axis],
+        )
+
+    def step(self, axis):
+        self.copy(axis).wait()
+        self.values[axis + 1] = self.values[axis] + self.landing[axis]
+        if axis < CORE:
+            self.copy(axis + 1).start()
+
+
+def complete(values):
+    lane = lax.broadcasted_iota(jnp.int32, values.shape, 1)
+    total = jnp.sum(values, axis=1, keepdims=True)
+    return jnp.where(lane == values.shape[1] - 1, -total, values)
+
+
+def widen(values):
+    return jnp.concatenate([values, jnp.zeros((values.shape[0], 1), values.dtype)], axis=1)
+
+
+def spread(shards, device):
+    count = shards.shape[1]
+    unit = count // 8
+    lane = lax.broadcasted_iota(jnp.int32, (1, count), 1)
+    flat = lane + device * unit
+    flat = jnp.where(lane >= unit, flat - unit + D, flat)
+    flat = jnp.where(lane >= 2 * unit, lane - 2 * unit + 2 * D + device * 2 * unit, flat)
+    flat = jnp.where(lane >= 4 * unit, lane - 4 * unit + 4 * D + device * 4 * unit, flat)
+    row = lax.broadcasted_iota(jnp.int32, (8, count), 0)
+    inside = flat - row * D
+    mine = jnp.where((inside >= 0) & (inside < D), shards, 0.0)
+    for _ in range(7):
+        flat = jnp.where(flat >= D, flat - D, flat)
+    column = lax.broadcasted_iota(jnp.int32, (D, count), 0)
+    place = jnp.where(column == flat, 1.0, 0.0)
+    return dot(mine.astype(bf16), place.astype(bf16), NT)
+
+
+def inverse_size(full):
+    return lax.rsqrt(jnp.mean(full * full, axis=1, keepdims=True) + norm_eps)
+
+
+def norm_backward(grad, full, inverse, gain):
+    scaled = grad * gain
+    inner = jnp.sum(scaled * full, axis=1, keepdims=True)
+    grad_full = scaled * inverse - full * (inverse * inverse * inverse * (inner * (1.0 / D)))
+    return grad * full * inverse, grad_full - grad_full[:, D - 1 : D]
+
+
+def gelu_and_slope(value):
+    square = value * value
+    bend = square * (gelu_root * 0.044715) + gelu_root
+    half = 0.5 * jnp.tanh(value * bend) + 0.5
+    act = value * half
+    return act, half + act * (1.0 - half) * (6.0 * bend - 4.0 * gelu_root)
+
+
+def norm_rows(rows, resid, gain, normed):
+    full = complete(widen(resid[rows, :].astype(f32)))
+    normed[rows, :] = (full * inverse_size(full) * gain).astype(bf16)
+
+
+def project(group, normed, qkv_w, small, qkv):
+    columns = pl.ds(aligned(group * GROUP, GROUP), GROUP)
+
+    def body(part, carry):
+        weight = qkv_w[part, :, :, :, :, :, columns].reshape(D, GROUP)
+        bias = jnp.where(part == 1, 0.0, small[pl.ds(2 + lax.div(part, 2), 1), columns])
+        qkv[:, pl.ds(aligned(part * D + group * GROUP, GROUP), GROUP)] = (
+            dot(normed[...], weight) + bias
+        ).astype(bf16)
+        return carry
+
+    lax.fori_loop(0, 3, body, 0)
+
+
+def pair_columns(pair):
+    return tuple(pl.ds(aligned(part * D + pair * LANES, LANES), LANES) for part in range(3))
+
+
+def pair_forward(pair, block, cross, qkv, mixed, mixed_rest, lse):
+    count = qkv.shape[0]
+    lane = lax.broadcasted_iota(jnp.int32, (ROWS, LANES), 1)
+    row = lax.broadcasted_iota(jnp.int32, (ROWS, ROWS), 0)
+    column = lax.broadcasted_iota(jnp.int32, (ROWS, ROWS), 1)
+    rows = pl.ds(block * ROWS, ROWS)
+    last = (block + 1) * ROWS
+    query_columns, key_columns, value_columns = pair_columns(pair)
+    query = qkv[rows, query_columns] * jnp.asarray(HD**-0.5, bf16)
+    key = qkv[pl.ds(0, last), key_columns]
+    value = qkv[pl.ds(0, last), value_columns]
+    value = jnp.concatenate([value, jnp.ones((last, LANES), bf16)], axis=1)
+    outs = []
+    stats = lse[rows, :]
+    for head in range(2):
+        mine = lane < HD if head == 0 else lane >= HD
+        scores = dot(jnp.where(mine, query, jnp.zeros_like(query)), key, NT)
+        parts = []
+        for other in range(block + 1):
+            part = scores[:, other * ROWS : (other + 1) * ROWS]
+            if other == block:
+                part = jnp.where(row >= column, part, masked_score)
+            elif block * ROWS >= count // 2 and other * ROWS < count // 2:
+                part = part + cross
+            parts.append(part)
+        scores = jnp.concatenate(parts, axis=1) if block else parts[0]
+        largest = jnp.max(scores, axis=1, keepdims=True)
+        summed = dot(jnp.exp(scores - largest).astype(bf16), value)
+        outs.append(summed[:, :LANES] / summed[:, LANES:])
+        stats = jnp.where(lane == 2 * pair + head, largest + jnp.log(summed[:, LANES:]), stats)
+    lse[rows, :] = stats
+    out = jnp.where(lane < HD, outs[0], outs[1])
+    low = out.astype(bf16)
+    mixed[rows, query_columns] = low
+    mixed_rest[rows, query_columns] = (out - low.astype(f32)).astype(bf16)
+
+
+def middle_rows(rows, resid, mixed, out_w, biases):
+    branch = dot(mixed[rows, :], out_w[...].reshape(D, D))
+    return widen(resid[rows, :].astype(f32)) + branch + biases[pl.ds(0, 1), :]
+
+
+def feed_normed_rows(rows, resid, mixed, small, biases, out_w, normed, normed_t):
+    full = complete(middle_rows(rows, resid, mixed, out_w, biases))
+    values = (full * inverse_size(full) * small[pl.ds(1, 1), :]).astype(bf16)
+    normed[rows, :] = values
+    normed_t[:, rows] = jnp.transpose(values)
+
+
+def feed_forward_columns(part, normed, small, up_w, activated, slopes):
+    columns = pl.ds(aligned(part * GROUP, GROUP), GROUP)
+    up = up_w[:, :, :, :, :, columns].reshape(D, GROUP)
+    bias = small[pl.ds(4 + lax.div(part, GROUPS), 1), pl.ds(aligned(lax.rem(part, GROUPS) * GROUP, GROUP), GROUP)]
+    act, slope = gelu_and_slope(dot(normed[...], up) + bias)
+    activated[:, columns] = act.astype(bf16)
+    slopes[:, columns] = slope.astype(bf16)
+
+
+def feed_backward_rows(
+    rows, starting, resid, cotangent, mixed, small, biases, weights, activated, grad_pre, keep, totals, sums, emit
+):
+    _, out_w, up_w, down_w = weights
+    branch, grad_mixed, whole_cotangent = keep
+    out, grad_normed = totals
+    cot = widen(cotangent[rows, :].astype(f32))
+    low_cot = cot.astype(bf16)
+    whole_cotangent[rows, :] = low_cot
+    middle = middle_rows(rows, resid, mixed, out_w, biases)
+    out[...] = middle + biases[pl.ds(1, 1), :]
+    grad_normed[...] = jnp.zeros(middle.shape, f32)
+
+    def body(part, carry):
+        columns = pl.ds(aligned(part * FF_BLOCK, FF_BLOCK), FF_BLOCK)
+        up = up_w[:, :, :, :, :, columns].reshape(D, FF_BLOCK)
+        down = down_w[lax.div(part, 2), lax.rem(part, 2)].reshape(FF_BLOCK, D)
+        grad = (dot(low_cot, down, NT) * grad_pre[rows, columns].astype(f32)).astype(bf16)
+        grad_pre[rows, columns] = grad
+        out[...] = out[...] + dot(activated[rows, columns], down)
+        grad_normed[...] = grad_normed[...] + dot(grad, up, NT)
+        total = column_sum(grad.astype(f32))
+        here = pl.ds(4 + part, 1)
+        sums[here, :] = jnp.where(starting, total, sums[here, :] + total)
+        return carry
+
+    lax.fori_loop(0, up_w.shape[-1] // FF_BLOCK, body, 0)
+    emit(out[...].astype(bf16))
+    full = complete(middle)
+    gain_terms, grad_input = norm_backward(
+        grad_normed[...], full, inverse_size(full), small[pl.ds(1, 1), :]
+    )
+    rounded = (cot + grad_input).astype(bf16)
+    branch[rows, :] = rounded
+    grad_mixed[rows, :] = dot(rounded, out_w[...].reshape(D, D), NT).astype(bf16)
+    for where, terms in ((1, gain_terms), (8, rounded.astype(f32)), (9, cot)):
+        total = column_sum(terms)
+        here = pl.ds(where, 1)
+        sums[here, :] = jnp.where(starting, total, sums[here, :] + total)
+
+
+def pair_backward(pair, block, cross, qkv, grad_mixed, lse_t, delta_t, grad_query):
+    count = qkv.shape[0]
+    lane = lax.broadcasted_iota(jnp.int32, (ROWS, LANES), 1)
+    row = lax.broadcasted_iota(jnp.int32, (ROWS, ROWS), 0)
+    column = lax.broadcasted_iota(jnp.int32, (ROWS, ROWS), 1)
+    keys = pl.ds(block * ROWS, ROWS)
+    queries = pl.ds(block * ROWS, count - block * ROWS)
+    query_columns, key_columns, value_columns = pair_columns(pair)
+    key = qkv[keys, key_columns] * jnp.asarray(HD**-0.5, bf16)
+    value = qkv[keys, value_columns]
+    query = qkv[queries, query_columns]
+    grad = grad_mixed[queries, query_columns]
+    grad_values = []
+    grad_keys = []
+    grad_queries = None
+    for head in range(2):
+        mine = lane < HD if head == 0 else lane >= HD
+        my_key = jnp.where(mine, key, jnp.zeros_like(key))
+        my_value = jnp.where(mine, value, jnp.zeros_like(value))
+        scores = dot(my_key, query, NT)
+        grad_probs = dot(my_value, grad, NT)
+        log_row = lse_t[pl.ds(2 * pair + head, 1), queries]
+        dot_row = delta_t[pl.ds(2 * pair + head, 1), queries]
+        probs = []
+        grad_scores = []
+        for other in range(count // ROWS - block):
+            span = slice(other * ROWS, (other + 1) * ROWS)
+            shifted = scores[:, span] - log_row[:, span]
+            if other == 0:
+                shifted = jnp.where(column >= row, shifted, masked_score)
+            elif block * ROWS < count // 2 and (block + other) * ROWS >= count // 2:
+                shifted = shifted + cross
+            prob = jnp.exp(shifted)
+            probs.append(prob.astype(bf16))
+            grad_scores.append((prob * (grad_probs[:, span] - dot_row[:, span])).astype(bf16))
+        probs = jnp.concatenate(probs, axis=1) if len(probs) > 1 else probs[0]
+        grad_scores = jnp.concatenate(grad_scores, axis=1) if len(grad_scores) > 1 else grad_scores[0]
+        grad_values.append(dot(probs, grad))
+        grad_keys.append(dot(grad_scores, query))
+        part = dot(grad_scores, my_key, TN)
+        grad_queries = part if grad_queries is None else grad_queries + part
+    qkv[keys, value_columns] = jnp.where(lane < HD, grad_values[0], grad_values[1]).astype(bf16)
+    qkv[keys, key_columns] = (
+        jnp.where(lane < HD, grad_keys[0], grad_keys[1]) * HD**-0.5
+    ).astype(bf16)
+    if block == 0:
+        grad_query[...] = grad_queries
+    else:
+        grad_query[queries, :] = grad_query[queries, :] + grad_queries
+
+
+def backward_rows(mixed, mixed_rest, grad_mixed, lse, lse_t, delta_t):
+    heads = lse_t.shape[0]
+    lse_t[...] = jnp.transpose(lse[...])[:heads]
+    head = lax.broadcasted_iota(jnp.int32, (heads, D), 0)
+    column = lax.broadcasted_iota(jnp.int32, (heads, D), 1)
+    pick = jnp.where((column >= head * HD) & (column < head * HD + HD), 1.0, 0.0).astype(f32)
+
+    def body(block, carry):
+        rows = pl.ds(aligned(block * ROWS, ROWS), ROWS)
+        whole = mixed[rows, :].astype(f32) + mixed_rest[rows, :].astype(f32)
+        product = whole * grad_mixed[rows, :].astype(f32)
+        delta_t[:, rows] = lax.dot_general(
+            pick, product, NT, precision=lax.Precision.HIGHEST, preferred_element_type=f32
+        )
+        return carry
+
+    lax.fori_loop(0, mixed.shape[0] // ROWS, body, 0)
+
+
+def layer_kernel(
+    resid, cotangent, qkv_in, out_in, up_in, down_in, small_in, biases_in, lengths,
+    out_resid, grad_resid, qkv_out, out_out, up_out, down_out, small_out, qkv_away,
+    *scratch,
+):
+    scratch = list(scratch)
+    take = lambda n: [scratch.pop(0) for _ in range(n)]
+    weights = take(4)
+    qkv_w, out_w, up_w, down_w = weights
+    landings = [take(CHIP_AXES + 1) for _ in range(CHUNKS)]
+    normed, qkv, mixed, mixed_rest, grad_mixed, branch, lse, staging = take(8)
+    my_rows, pair_rows, biases, small_values, small_landing, sum_values, sum_landing = take(7)
+    (
+        pair_send, pair_recv, small_send, small_recv, sum_send, sum_recv,
+        gather_send, gather_recv, reduce_send, reduce_recv,
+        final_send, final_recv, final_own, row_sems,
+    ) = take(14)
+    activated = qkv
+    qkv = activated.at[:, pl.ds(0, 3 * D)]
+    count = resid.shape[0]
+    place = Place()
+    core = place.core
+    cross = jnp.where(lengths[0, 0] == count, 0.0, masked_score)
+    enter(place)
+
+    shards = (qkv_in, out_in, up_in)
+    shard_rows = BLOCK // 2
+    offsets = ((0, 0), (0, qkv_in.shape[1]), (shard_rows, 0))
+    for shard, (top, left) in zip(shards, offsets):
+        values = shard[...].astype(f32)
+        values = widen(values) if values.shape[1] == D - 1 else values
+        my_rows[pl.ds(top, shard_rows), pl.ds(left, values.shape[1])] = values
+    pair_copy = send(place, CORE, my_rows, pair_rows, pair_send.at[0], pair_recv.at[0])
+    pair_copy.start()
+    small_values[0] = spread(small_in[...], place.wide * 4 + place.narrow)
+    small_sum = SmallSum(place, small_values, small_landing, small_send, small_recv)
+    small_sum.copy(0).start()
+    biases[...] = widen(biases_in[...])
+
+    def own_block(slot, first, width):
+        top, left = offsets[slot]
+        here = (pl.ds(top, shard_rows), pl.ds(aligned(left + first, LANES), width))
+        mine, theirs = my_rows[here], pair_rows[here]
+        return jnp.concatenate(
+            [jnp.where(core == 0, mine, theirs), jnp.where(core == 0, theirs, mine)], axis=0
+        ).astype(bf16)
+
+    here = place.region()
+    gathers = [
+        GatherChunk(place, GATHER_ORDERS[index], view, gather_send.at[index], gather_recv.at[index])
+        for index, (view, _, _) in enumerate(weight_chunks(weights))
+    ]
+    down_w[here + (core,)] = widen(down_in[...].astype(f32)).astype(bf16)
+    pair_copy.wait()
+    for group in range(GROUPS):
+        for part in range(3):
+            first = group * GROUP + core * LANES
+            qkv_w[(part,) + here + (slice(None), pl.ds(aligned(first, LANES), LANES))] = own_block(
+                0, part * D + first, LANES
+            )
+    opening = list(GATHER_STEPS["FIRST"])
+    while opening[0] in ((Q0, 0), (Q1, 0), (Q2, 0)):
+        gathers[opening.pop(0)[0]].step(0)
+    for slot, whole in ((1, out_w), (2, up_w)):
+        half = whole.shape[-1] // 2
+        first = aligned(core * half, LANES)
+        whole[here + (slice(None), pl.ds(first, half))] = own_block(slot, first, half)
+
+    lse[...] = jnp.zeros_like(lse)
+
+    def norm_all():
+        def body(block, carry):
+            norm_rows(
+                pl.ds(aligned(block * ROWS, ROWS), ROWS), resid, small_values[5][0:1], normed
+            )
+            return carry
+
+        lax.fori_loop(0, count // ROWS, body, 0)
+
+    axis = 0
+    for number, (chunk, stage) in enumerate(opening):
+        if (chunk, stage) == (Q0, 5):
+            norm_all()
+        gathers[chunk].step(stage)
+        while axis <= CORE and (axis + 1) * (opening.index((Q0, 4)) + 1) <= (number + 1) * 5:
+            small_sum.step(axis)
+            axis += 1
+
+    small = small_values.at[5]
+    save = pltpu.make_async_copy(qkv, qkv_away, row_sems.at[4])
+    blocks = count // ROWS
+    pairs = H // 2
+    per_group = pairs // GROUPS
+    ticks = GATHER_STEPS["FORWARD"]
+    after_up = GATHER_STEPS["FEED"]
+
+    def gather_steps(where):
+        for chunk, stage in GATHER_STEPS[where]:
+            gathers[chunk].step(stage)
+
+    def after(number, index, steps_of, run):
+        for which in range(number):
+            steps = steps_of(which)
+            if steps:
+                @pl.when(index == which)
+                def _():
+                    for chunk, stage in steps:
+                        run(chunk, stage)
+
+    def forward(pair, carry):
+        @pl.when(lax.rem(pair, per_group) == 0)
+        def _():
+            project(lax.div(pair, per_group), normed, qkv_w, small, qkv)
+
+        @pl.when(pair == pairs - per_group)
+        def _():
+            save.start()
+
+        for block in range(blocks):
+            pair_forward(pair, block, cross, qkv, mixed, mixed_rest, lse)
+            if (block + 1) * TICKS % blocks == 0:
+                turn = (block + 1) * TICKS // blocks - 1
+                after(
+                    pairs, pair, lambda which: ticks[which * TICKS + turn],
+                    lambda chunk, stage: gathers[chunk].step(stage),
+                )
+        return carry
+
+    lax.fori_loop(0, pairs, forward, 0)
+    save.wait()
+
+    sums = sum_values.at[0]
+    sums[...] = jnp.zeros(sums.shape, f32)
+    reduces = [
+        ReduceChunk(
+            place, REDUCE_ORDERS[index], view, (slice(None),) * len(lead),
+            landings[index], reduce_send.at[index], reduce_recv.at[index],
+        )
+        for index, (view, lead, _) in enumerate(weight_chunks(weights))
+    ]
+
+    def emit_rows(target, block, sem, values):
+        rows = pl.ds(aligned(block * ROWS, ROWS), ROWS)
+
+        @pl.when(block > 0)
+        def _():
+            pltpu.make_async_copy(staging, target.at[rows, :], sem).wait()
+
+        staging[...] = values
+        pltpu.make_async_copy(staging, target.at[rows, :], sem).start()
+
+    def emit_last(target, sem):
+        pltpu.make_async_copy(staging, target.at[pl.ds(0, ROWS), :], sem).wait()
+
+    def feed_forward(grad_pre, whole_cotangent, normed_t, out_total, grad_total):
+        def normed_body(block, carry):
+            rows = pl.ds(aligned(block * ROWS, ROWS), ROWS)
+            feed_normed_rows(rows, resid, mixed, small, biases, out_w, grad_mixed, normed_t)
+            return carry
+
+        gather_steps("NORMED")
+        lax.fori_loop(0, blocks, normed_body, 0)
+        gather_steps("UP")
+
+        def there(part, carry):
+            feed_forward_columns(part, grad_mixed, small, up_w, activated, grad_pre)
+            after(
+                len(after_up), part, lambda which: after_up[which],
+                lambda chunk, stage: gathers[chunk].step(stage),
+            )
+            return carry
+
+        lax.fori_loop(0, len(after_up), there, 0)
+        gather_steps("BACK")
+        for chunk in gathers:
+            chunk.drain()
+
+        def back(block, carry):
+            rows = pl.ds(aligned(block * ROWS, ROWS), ROWS)
+            feed_backward_rows(
+                rows, block == 0, resid, cotangent, mixed, small, biases, weights, activated,
+                grad_pre, (branch, grad_mixed, whole_cotangent), (out_total, grad_total), sums,
+                partial(emit_rows, out_resid, block, row_sems.at[1]),
+            )
+            return carry
+
+        lax.fori_loop(0, blocks, back, 0)
+
+        def grad_down(part, carry):
+            columns = pl.ds(aligned(part * FF_BLOCK, FF_BLOCK), FF_BLOCK)
+            down_w[lax.div(part, 2), lax.rem(part, 2)] = (
+                dot(activated[:, columns], whole_cotangent[...], TN)
+                .astype(bf16)
+                .reshape(down_w.shape[2:])
+            )
+            return carry
+
+        lax.fori_loop(0, up_w.shape[-1] // FF_BLOCK, grad_down, 0)
+        reduces[DOWN_A].launch(0)
+        reduces[DOWN_B].launch(0)
+        pltpu.make_async_copy(qkv_away, qkv, row_sems.at[4]).start()
+
+        def grad_up(part, carry):
+            columns = pl.ds(aligned(part * FF_BLOCK, FF_BLOCK), FF_BLOCK)
+            up_w[:, :, :, :, :, columns] = (
+                dot(normed_t[...], grad_pre[:, columns])
+                .astype(bf16)
+                .reshape((2,) * CHIP_AXES + (BLOCK, FF_BLOCK))
+            )
+            after(
+                len(REDUCE_STEPS["GRAD_UP"]), part, lambda which: REDUCE_STEPS["GRAD_UP"][which],
+                lambda chunk, stage: reduces[chunk].absorb(stage),
+            )
+            return carry
+
+        lax.fori_loop(0, up_w.shape[-1] // FF_BLOCK, grad_up, 0)
+        reduces[UP_A].launch(0)
+        reduces[UP_B].launch(0)
+
+        def grad_out(half, carry):
+            columns = pl.ds(aligned(half * (D // 2), LANES), D // 2)
+            out_w[half] = (
+                dot(mixed[:, columns], branch[...], TN).astype(bf16).reshape(out_w.shape[1:])
+            )
+            return carry
+
+        lax.fori_loop(0, 2, grad_out, 0)
+        reduces[OUT].launch(0)
+        emit_last(out_resid, row_sems.at[1])
+
+    pl.run_scoped(
+        feed_forward,
+        pltpu.VMEM((count, up_w.shape[-1]), bf16),
+        pltpu.VMEM((count, D), bf16),
+        pltpu.VMEM((D, count), bf16),
+        pltpu.VMEM((ROWS, D), f32),
+        pltpu.VMEM((ROWS, D), f32),
+    )
+    pltpu.make_async_copy(qkv_away, qkv, row_sems.at[4]).wait()
+
+    def reduce_steps(where):
+        for chunk, stage in REDUCE_STEPS[where]:
+            reduces[chunk].absorb(stage)
+
+    def attention_backward(grad_normed, lse_t, delta_t, grad_query, normed_t):
+        def turn(block, carry):
+            rows = pl.ds(aligned(block * ROWS, ROWS), ROWS)
+            normed_t[:, rows] = jnp.transpose(normed[rows, :])
+            grad_normed[rows, :] = jnp.zeros((ROWS, D), f32)
+            return carry
+
+        lax.fori_loop(0, blocks, turn, 0)
+        backward_rows(mixed, mixed_rest, grad_mixed, lse, lse_t, delta_t)
+        reduce_steps("PREPARED")
+        ticks = REDUCE_STEPS["BACKWARD"]
+
+        def finish_group(group):
+            columns = pl.ds(aligned(group * GROUP, GROUP), GROUP)
+
+            def grad_columns(part):
+                return pl.ds(aligned(part * D + group * GROUP, GROUP), GROUP)
+
+            def of_rows(block, carry):
+                rows = pl.ds(aligned(block * ROWS, ROWS), ROWS)
+                total = grad_normed[rows, :]
+                for part in range(3):
+                    weight = qkv_w[part, :, :, :, :, :, columns].reshape(D, GROUP)
+                    total = total + dot(qkv[rows, grad_columns(part)], weight, NT)
+                grad_normed[rows, :] = total
+                return carry
+
+            lax.fori_loop(0, blocks, of_rows, 0)
+
+            def of_weight(part, carry):
+                grads = qkv[:, grad_columns(part)]
+                qkv_w[part, :, :, :, :, :, columns] = (
+                    dot(normed_t[...], grads)
+                    .astype(bf16)
+                    .reshape((2,) * CHIP_AXES + (BLOCK, GROUP))
+                )
+                here = jnp.where(part == 1, 10, 2 + lax.div(part, 2))
+                sums[pl.ds(here, 1), columns] = column_sum(grads.astype(f32))
+                return carry
+
+            lax.fori_loop(0, 3, of_weight, 0)
+
+        def backward(pair, carry):
+            for block in range(blocks):
+                pair_backward(pair, block, cross, qkv, grad_mixed, lse_t, delta_t, grad_query)
+                if (block + 1) * TICKS % blocks == 0:
+                    turn = (block + 1) * TICKS // blocks - 1
+                    after(
+                        pairs, pair, lambda which: ticks[which * TICKS + turn],
+                        lambda chunk, stage: reduces[chunk].absorb(stage),
+                    )
+            qkv[:, pair_columns(pair)[0]] = grad_query[...].astype(bf16)
+
+            @pl.when(lax.rem(pair, per_group) == per_group - 1)
+            def _():
+                finish_group(lax.div(pair, per_group))
+
+            def finished(chunk, stage):
+                if stage is None:
+                    reduces[chunk].launch(0)
+                else:
+                    reduces[chunk].absorb(stage)
+
+            def steps_of(which):
+                if which % per_group < per_group - 1:
+                    return []
+                group = which // per_group
+                return [(group, None)] + REDUCE_STEPS["FINISHED"][group]
+
+            after(pairs, pair, steps_of, finished)
+            return carry
+
+        lax.fori_loop(0, pairs, backward, 0)
+
+        def body(block, carry):
+            rows = pl.ds(aligned(block * ROWS, ROWS), ROWS)
+            full = complete(widen(resid[rows, :].astype(f32)))
+            gain_terms, grad_input = norm_backward(
+                grad_normed[rows, :], full, inverse_size(full), small[pl.ds(0, 1), :]
+            )
+            emit_rows(
+                grad_resid, block, row_sems.at[2],
+                (branch[rows, :].astype(f32) + grad_input).astype(bf16),
+            )
+            total = column_sum(gain_terms)
+            sums[pl.ds(0, 1), :] = jnp.where(block == 0, total, sums[pl.ds(0, 1), :] + total)
+            return carry
+
+        lax.fori_loop(0, count // ROWS, body, 0)
+
+    pl.run_scoped(
+        attention_backward,
+        pltpu.VMEM((count, D), f32),
+        pltpu.VMEM((16, count), f32),
+        pltpu.VMEM((16, count), f32),
+        pltpu.VMEM((count, LANES), f32),
+        pltpu.VMEM((D, count), bf16),
+    )
+    sum_all = SmallSum(place, sum_values, sum_landing, sum_send, sum_recv)
+    sum_all.copy(0).start()
+    reduce_steps("NORM")
+    rest = REDUCE_STEPS["REST"]
+    axis = 0
+    for number, (chunk, stage) in enumerate(rest):
+        reduces[chunk].absorb(stage)
+        if axis < CORE:
+            sum_all.step(axis)
+            axis += 1
+    while axis <= CORE:
+        sum_all.step(axis)
+        axis += 1
+    small_out[...] = sum_values[5]
+
+    for chunk, start in ((DOWN_A, 0), (DOWN_B, D // 2)):
+        down_out[:, pl.ds(start, D // 2)] = reduces[chunk].total()
+    their_rows = pl.ds(aligned((1 - core) * shard_rows, 8), shard_rows)
+    kept_rows = pl.ds(aligned(core * shard_rows, 8), shard_rows)
+    copies = []
+
+    def deliver(slot, part_of, target):
+        away = send(
+            place, CORE, part_of(their_rows), target, final_send.at[slot], final_recv.at[slot]
+        )
+        away.start()
+        home = pltpu.make_async_copy(part_of(kept_rows), target, final_own.at[slot])
+        home.start()
+        copies.extend((away, home))
+
+    finals = pair_rows
+    half = up_w.shape[-1] // 4
+    finals[:, pl.ds(0, half)] = reduces[UP_A].total()
+    finals[:, pl.ds(half, half)] = reduces[UP_B].total()
+    deliver(
+        0, lambda rows: finals.at[rows, pl.ds(0, 2 * half)],
+        up_out.at[:, pl.ds(aligned(core * 2 * half, LANES), 2 * half)],
+    )
+    first = 2 * half
+    finals[:, pl.ds(first, D // 2)] = reduces[OUT].total()
+    deliver(
+        1, lambda rows: finals.at[rows, pl.ds(2 * half, D // 2)],
+        out_out.at[:, pl.ds(aligned(core * (D // 2), LANES), D // 2)],
+    )
+    first += D // 2
+    for group in range(GROUPS):
+        total = reduces[group].total()
+        for part in range(3):
+            here = pl.ds(first, LANES)
+            finals[:, here] = total[part]
+            deliver(
+                2 + group * 3 + part, lambda rows, here=here: finals.at[rows, here],
+                qkv_out.at[:, pl.ds(aligned(part * D + group * GROUP + core * LANES, LANES), LANES)],
+            )
+            first += LANES
+    for copy in copies:
+        copy.wait()
+    for chunk in reduces:
+        chunk.drain()
+    emit_last(grad_resid, row_sems.at[2])
+
+
+def layer_by_kernel(resid, cotangent, qkv_in, out_in, up_in, down_in, small_in, biases, lengths):
+    count = resid.shape[0]
+    grid = (2,) * CHIP_AXES
+    ff = up_in.shape[1]
+    weight_shapes = [
+        (3,) + grid + (BLOCK, D),
+        grid + (BLOCK, D),
+        grid + (BLOCK, ff),
+        grid + (2, down_in.shape[0], D),
+    ]
+    weights = [pltpu.VMEM(shape, bf16) for shape in weight_shapes]
+    shapes = [jax.ShapeDtypeStruct(shape, bf16) for shape in weight_shapes]
+    landings = [
+        pltpu.VMEM(lead + (2,) * (CHIP_AXES - stage) + block, bf16)
+        for _, lead, block in weight_chunks(shapes)
+        for stage in range(CHIP_AXES + 1)
+    ]
+    dma = pltpu.SemaphoreType.DMA
+    small_rows, sum_rows = 8, 16
+    scratch = (
+        weights
+        + landings
+        + [
+            pltpu.VMEM((count, D), bf16),
+            pltpu.VMEM((count, ff), bf16),
+            pltpu.VMEM((count, D), bf16),
+            pltpu.VMEM((count, D), bf16),
+            pltpu.VMEM((count, D), bf16),
+            pltpu.VMEM((count, D), bf16),
+            pltpu.VMEM((count, LANES), f32),
+            pltpu.VMEM((ROWS, D), bf16),
+            pltpu.VMEM((BLOCK, (3 * D + D + ff) // 2), f32),
+            pltpu.VMEM((BLOCK, (3 * D + D + ff) // 2), f32),
+            pltpu.VMEM((2, D), f32),
+            pltpu.VMEM((6, small_rows, D), f32),
+            pltpu.VMEM((5, small_rows, D), f32),
+            pltpu.VMEM((6, sum_rows, D), f32),
+            pltpu.VMEM((5, sum_rows, D), f32),
+            dma((3,)),
+            dma((3,)),
+            dma((5,)),
+            dma((5,)),
+            dma((5,)),
+            dma((5,)),
+            dma((CHUNKS, GATHER_COPIES)),
+            dma((CHUNKS, GATHER_COPIES)),
+            dma((CHUNKS, CHIP_AXES + 1)),
+            dma((CHUNKS, CHIP_AXES + 1)),
+            dma((11,)),
+            dma((11,)),
+            dma((11,)),
+            dma((5,)),
+        ]
+    )
+    in_vmem = pl.BlockSpec(memory_space=pltpu.VMEM)
+    in_hbm = pl.BlockSpec(memory_space=pl.ANY)
+    shard_rows = BLOCK // 2
+    return pl.pallas_call(
+        layer_kernel,
+        out_shape=[
+            jax.ShapeDtypeStruct((count, D), bf16),
+            jax.ShapeDtypeStruct((count, D), bf16),
+            jax.ShapeDtypeStruct((shard_rows, 3 * D), f32),
+            jax.ShapeDtypeStruct((shard_rows, D), f32),
+            jax.ShapeDtypeStruct((shard_rows, ff), f32),
+            jax.ShapeDtypeStruct((down_in.shape[0], D), f32),
+            jax.ShapeDtypeStruct((sum_rows, D), f32),
+            jax.ShapeDtypeStruct((count, 3 * D), bf16),
+        ],
+        in_specs=[in_vmem] * 8 + [pl.BlockSpec(memory_space=pltpu.SMEM)],
+        out_specs=[in_hbm] * 2 + [in_vmem] * 5 + [in_hbm],
+        scratch_shapes=scratch,
+        compiler_params=pltpu.CompilerParams(
+            collective_id=1, has_side_effects=True, vmem_limit_bytes=VMEM_BYTES
+        ),
+        name="layer",
+    )(resid, cotangent, qkv_in, out_in, up_in, down_in, small_in, biases, lengths)
+
+
+VMEM_BYTES = 63 * 2**20
+
+
+def device_index():
+    return lax.axis_index("wide") * lax.axis_size("narrow") + lax.axis_index("narrow")
+
+
+def on_device_by_kernel(
+    resid, gain_attn, qkv_weight, qv_bias, out_weight, out_bias, gain_mlp,
+    up_weight, up_bias, down_weight, down_bias, cotangent, seq_lengths,
+):
+    devices = lax.axis_size("wide") * lax.axis_size("narrow")
+    width = out_weight.shape[1]
+    small = jnp.concatenate([gain_attn, gain_mlp, qv_bias, up_bias]).astype(f32)
+    biases = jnp.stack([out_bias, down_bias]).astype(f32)
+    out_resid, grad_resid, qkv, out, up, down, sums, _ = layer_by_kernel(
+        resid, cotangent, qkv_weight, out_weight, up_weight, down_weight,
+        small.reshape(1, -1), biases, seq_lengths,
+    )
+    sums = sums.reshape(-1)
+
+    def shard(first, count):
+        part = count // devices
+        return lax.dynamic_slice(sums, (first + device_index() * part,), (part,))
+
+    ff = up_weight.shape[1]
+    last = 4 * D + ff
+    return (
+        out_resid[:, :width],
+        grad_resid[:, :width],
+        shard(0, D),
+        qkv,
+        shard(2 * D, 2 * D),
+        out[:, :width],
+        sums[last : last + width],
+        shard(D, D),
+        up,
+        shard(4 * D, ff),
+        down[:, :width],
+        sums[last + D : last + D + width],
+    )
 
 
 def compressed_norm(values, gain_vec):
@@ -185,16 +1220,7 @@
         + jnp.dot(mlp_first[2], gathered[3], preferred_element_type=jnp.float32)
         + down_bias.astype(jnp.float32)
     ).astype(jnp.bfloat16)
-    weights_back = (
-        lax.all_gather(shards[0], ("wide", "narrow"), axis=0, tiled=True),
-        lax.all_gather(shards[1], ("wide", "narrow"), axis=0, tiled=True),
-        lax.all_gather(shards[2], ("wide", "narrow"), axis=0, tiled=True),
-        lax.all_gather(shards[3], ("wide", "narrow"), axis=0, tiled=True),
-        lax.all_gather(shards[4], ("wide", "narrow"), axis=0, tiled=True),
-        lax.all_gather(shards[5], ("wide", "narrow"), axis=0, tiled=True),
-        lax.all_gather(shards[6], ("wide", "narrow"), axis=0, tiled=True),
-        lax.all_gather(shards[7], ("wide", "narrow"), axis=0, tiled=True),
-    )
+    weights_back = gathered
     normed_mlp, pre_act, activated = mlp_part(middle, weights_back)
     grad_out = cotangent.astype(jnp.float32)
     grad_w_down = contract_rows(activated, cotangent)
@@ -265,8 +1291,9 @@
 
 
 def solution(mesh):
+    by_kernel = mesh.shape["wide"] == 8 and mesh.shape["narrow"] == 4
     return jax.shard_map(
-        on_device,
+        on_device_by_kernel if by_kernel else on_device,
         mesh=mesh,
         in_specs=(
             P(("wide", "narrow"), None),

time: 836 us -> 217 us (0.26)
  waiting for transfers between devices: 444 us -> 0 us
  Pallas kernels: 0 us -> 203 us
  matrix products: 197 us -> 0 us
  blocking collectives: 84.5 us -> 0 us
  other arithmetic: 55.2 us -> 1.95 us
  local copies, waits for them, and re-layouts: 36.7 us -> 11.2 us
  between operations: 15.2 us -> 0.68 us
    reduce_scatter x4 -> x0, waiting for transfers between devices: 333 us -> none  [the longest x1 142 us: on_device(): lax.psum_scatter(grad_w_up, ('wide', 'narrow'), scatter_dimension=0, tile...]
    pallas_call x0 -> x1, Pallas kernels: none -> 203 us  [layer_by_kernel(): pl.pallas_call(layer_kernel, out_shape=[jax.ShapeDtypeStruct((count, D),...]
    dot_general x24 -> x0, matrix products: 197 us -> none  [the longest x4 33.7 us: contract_rows(): lax.dot_general(left_side, right_side, (((0,), (0,)), ((), ())), preferre...]
    all_gather x4 -> x0, waiting for transfers between devices: 108 us -> none  [the longest x1 54.3 us: on_device(): lax.all_gather(shards[3], ('wide', 'narrow'), axis=0, tiled=True)]
    unnamed x2 -> x0, blocking collectives: 84.5 us -> none
    convert_element_type x8 -> x2, other arithmetic: 27.4 us -> 1.95 us  [the longest x1 1.34 us: on_device_by_kernel(): small = jnp.concatenate([gain_attn, gain_mlp, qv_bias, up_bias]).astype(f32)]
    reduce_sum x9 -> x0, other arithmetic: 20.5 us -> none  [the longest x2 14.7 us: attend_forward(): summed = jnp.sum(exp_scores, axis=-1, keepdims=True)]
    unnamed x134 -> x16, local copies, waits for them, and re-layouts: 22 us -> 6.68 us
  transfers between devices with their start and end apart: 8 -> 0, of which waited for: 6 -> 0; matrix products, arithmetic and copies ran while one was open for 27% -> 0% of each run, Pallas kernels for 0% -> 0%
where the time goes in v2:
time: 217 us
  Pallas kernels  203 us (94%)
  local copies, waits for them, and re-layouts  11.2 us (5%)
    pallas_call x1, Pallas kernels, layer_by_kernel(): pl.pallas_call(layer_kernel, out_shape=[jax.ShapeDtypeStruct((count, D),...  203 us
    unnamed x16, local copies, waits for them, and re-layouts  6.68 us

profile of v2, /device:TPU:0, one launch (start us, length us, event | category | flops | bytes accessed | tf_op | source)
XLA Modules:
  0.0 216.9 jit_solution(850576827982709531)
XLA Ops:
  0.6 1.3 maximum_convert_fusion.1.small_in
  2.0 0.7 stack.10
  2.7 0.7 stack.9
  3.4 0.6 maximum_convert_fusion.biases_in
  4.0 203.1 %layer.1 = (bf16[1024,768]{1,0:T(8,128)(2,1)}, bf16[1024,768]{1,0:T(8,128)(2,1)}, f32[24,2304]{1,0:T(8,128)}, f32[24,768]{1,0:T(8,128)}, f32[24,3072]{1,0:T(8,12...) custom-call(bf16[1024,767]{1,0:T(8,128)(2,1)} %resid.1, bf16[1024,767]{1,0:T(8,128)(2,1)} %cotangent.1, ...), custom_call_target="tpu_custom_call" | custom-call | tf_op jit(solution)/shard_map/layer/pallas_call | solution.py:987
  207.1 0.8 reshape.83
  207.9 0.6 fusion.1
  208.4 0.6 dynamic_slice.13
  209.0 0.6 fusion
  209.6 0.6 dynamic_slice.15
  210.2 0.0 copy-start
  210.2 2.8 %copy.31 = bf16[1024,767]{1,0:T(8,128)(2,1)} copy(bf16[1024,767]{1,0:T(8,128)(2,1)} %bitcast.9) | data formatting | bytes 3141632
  213.0 0.0 copy-done
  213.0 0.0 copy-start.3
  213.0 0.0 copy-start.4
  213.0 0.0 copy-start.2
  213.0 0.0 copy-start.1
  213.0 1.1 copy.32
  214.2 0.0 copy-done.3
  214.2 0.7 copy.33
  214.8 0.0 copy-done.4
  214.8 0.6 copy.34
  215.5 0.0 copy-done.2
  215.5 0.7 copy.35
  216.2 0.0 copy-done.1
  216.2 0.7 copy.36
Async XLA Ops:
  210.2 2.8 %copy-start = (bf16[1024,768]{1,0:T(8,128)(2,1)S(1)}, bf16[1024,768]{1,0:T(8,128)(2,1)}, u32[]{:S(2)}) copy-start(bf16[1024,768]{1,0:T(8,128)(2,1)} %get-tuple-element.20) | copy-start | bytes 4718596
  213.0 1.2 copy-start.3
  213.0 1.9 copy-start.4
  213.0 2.5 %copy-start.2 = (f32[24,3072]{1,0:T(8,128)S(1)}, f32[24,3072]{1,0:T(8,128)}, u32[]{:S(2)}) copy-start(f32[24,3072]{1,0:T(8,128)} %get-tuple-element.50) | copy-start | bytes 884740
  213.0 3.2 %copy-start.1 = (f32[96,768]{1,0:T(8,128)S(1)}, f32[96,768]{1,0:T(8,128)}, u32[]{:S(2)}) copy-start(f32[96,768]{1,0:T(8,128)} %get-tuple-element.25) | copy-start | bytes 884740

commit v3 on v2

--- a/solution.py
+++ b/solution.py
@@ -253,16 +253,20 @@
     "NORMED": [],
     "UP": [(UP_B, 5)],
     "FEED": [[], [(DOWN_A, 3)], [(DOWN_B, 3)], [], [], [], [], [], [], [], [(DOWN_A, 4)], [(DOWN_B, 4)]],
-    "BACK": [(DOWN_A, 5), (DOWN_B, 5)],
+    "GRAD_DOWN": [[], [(DOWN_A, 5), (DOWN_B, 5)], [], []],
+    "BACK": [],
 }
 
 REDUCE_STEPS = {
-    "GRAD_UP": [[], [], [(DOWN_A, 0)], [(DOWN_B, 0)]],
-    "PREPARED": [(UP_A, 0), (UP_B, 0), (OUT, 0)],
-    "BACKWARD": [[], [], [(DOWN_A, 1)], [(DOWN_B, 1)], [], [(Q0, 0)], [(UP_A, 1), (UP_B, 1)], [], [], [(Q0, 1), (Q1, 0), (DOWN_B, 3)], [(DOWN_A, 2)], [(UP_B, 2)]],
-    "FINISHED": [[], [(DOWN_B, 2), (OUT, 1)], [(DOWN_A, 3), (UP_A, 2), (OUT, 2)]],
-    "NORM": [(UP_B, 3), (Q0, 2), (Q2, 0)],
-    "REST": [(UP_A, 3), (Q1, 1), (OUT, 3), (Q0, 3), (Q2, 1), (Q1, 2), (Q2, 2), (Q1, 3), (Q2, 3)],
+    "STARTED": [(DOWN_A, 0)],
+    "BACK": [[(DOWN_B, 0)], [], [], []],
+    "GRAD_UP": [[(DOWN_A, 1)], [], [], [(DOWN_B, 1)]],
+    "PREPARED": [(UP_A, 0), (UP_B, 0), (OUT, 0), (DOWN_A, 2)],
+    "BACKWARD": [[], [(DOWN_B, 2)], [(DOWN_A, 3)], [], [(DOWN_B, 3)], [(Q0, 0)], [(UP_B, 1)], [(UP_A, 1)], [], [(Q0, 1), (Q1, 0), (OUT, 1)], [], []],
+    "FINISHED": [[], [], [(UP_A, 2), (UP_B, 2)]],
+    "RESID": [[], [(Q0, 2), (Q2, 0), (OUT, 2)], [(UP_A, 3)], []],
+    "OUT": [[(Q1, 1), (UP_B, 3)], [(Q0, 3)], [(Q2, 1), (OUT, 3)], []],
+    "REST": [(Q1, 2), (Q2, 2), (Q1, 3), (Q2, 3)],
 }
 
 
@@ -413,17 +417,11 @@
 
 
 def feed_backward_rows(
-    rows, starting, resid, cotangent, mixed, small, biases, weights, activated, grad_pre, keep, totals, sums, emit
+    rows, starting, resid, cotangent, mixed, small, biases, weights, grad_pre, branch, grad_mixed, grad_normed, sums
 ):
     _, out_w, up_w, down_w = weights
-    branch, grad_mixed, whole_cotangent = keep
-    out, grad_normed = totals
-    cot = widen(cotangent[rows, :].astype(f32))
-    low_cot = cot.astype(bf16)
-    whole_cotangent[rows, :] = low_cot
-    middle = middle_rows(rows, resid, mixed, out_w, biases)
-    out[...] = middle + biases[pl.ds(1, 1), :]
-    grad_normed[...] = jnp.zeros(middle.shape, f32)
+    low_cot = cotangent[rows, :]
+    grad_normed[...] = jnp.zeros(grad_normed.shape, f32)
 
     def body(part, carry):
         columns = pl.ds(aligned(part * FF_BLOCK, FF_BLOCK), FF_BLOCK)
@@ -431,7 +429,6 @@
         down = down_w[lax.div(part, 2), lax.rem(part, 2)].reshape(FF_BLOCK, D)
         grad = (dot(low_cot, down, NT) * grad_pre[rows, columns].astype(f32)).astype(bf16)
         grad_pre[rows, columns] = grad
-        out[...] = out[...] + dot(activated[rows, columns], down)
         grad_normed[...] = grad_normed[...] + dot(grad, up, NT)
         total = column_sum(grad.astype(f32))
         here = pl.ds(4 + part, 1)
@@ -439,11 +436,11 @@
         return carry
 
     lax.fori_loop(0, up_w.shape[-1] // FF_BLOCK, body, 0)
-    emit(out[...].astype(bf16))
-    full = complete(middle)
+    full = complete(middle_rows(rows, resid, mixed, out_w, biases))
     gain_terms, grad_input = norm_backward(
         grad_normed[...], full, inverse_size(full), small[pl.ds(1, 1), :]
     )
+    cot = low_cot.astype(f32)
     rounded = (cot + grad_input).astype(bf16)
     branch[rows, :] = rounded
     grad_mixed[rows, :] = dot(rounded, out_w[...].reshape(D, D), NT).astype(bf16)
@@ -451,6 +448,19 @@
         total = column_sum(terms)
         here = pl.ds(where, 1)
         sums[here, :] = jnp.where(starting, total, sums[here, :] + total)
+
+
+def feed_out_rows(rows, resid, mixed, biases, out_w, down_w, activated, total):
+    total[...] = middle_rows(rows, resid, mixed, out_w, biases) + biases[pl.ds(1, 1), :]
+
+    def body(part, carry):
+        columns = pl.ds(aligned(part * FF_BLOCK, FF_BLOCK), FF_BLOCK)
+        down = down_w[lax.div(part, 2), lax.rem(part, 2)].reshape(FF_BLOCK, D)
+        total[...] = total[...] + dot(activated[rows, columns], down)
+        return carry
+
+    lax.fori_loop(0, down_w.shape[0] * down_w.shape[1], body, 0)
+    return total[...].astype(bf16)
 
 
 def pair_backward(pair, block, cross, qkv, grad_mixed, lse_t, delta_t, grad_query):
@@ -492,7 +502,7 @@
         grad_scores = jnp.concatenate(grad_scores, axis=1) if len(grad_scores) > 1 else grad_scores[0]
         grad_values.append(dot(probs, grad))
         grad_keys.append(dot(grad_scores, query))
-        part = dot(grad_scores, my_key, TN)
+        part = dot(my_key, grad_scores, TN)
         grad_queries = part if grad_queries is None else grad_queries + part
     qkv[keys, value_columns] = jnp.where(lane < HD, grad_values[0], grad_values[1]).astype(bf16)
     qkv[keys, key_columns] = (
@@ -501,7 +511,7 @@
     if block == 0:
         grad_query[...] = grad_queries
     else:
-        grad_query[queries, :] = grad_query[queries, :] + grad_queries
+        grad_query[:, queries] = grad_query[:, queries] + grad_queries
 
 
 def backward_rows(mixed, mixed_rest, grad_mixed, lse, lse_t, delta_t):
@@ -525,7 +535,7 @@
 
 def layer_kernel(
     resid, cotangent, qkv_in, out_in, up_in, down_in, small_in, biases_in, lengths,
-    out_resid, grad_resid, qkv_out, out_out, up_out, down_out, small_out, qkv_away,
+    out_resid, grad_resid, qkv_out, out_out, up_out, down_out, small_out, qkv_away, rest_away, activated_away,
     *scratch,
 ):
     scratch = list(scratch)
@@ -533,7 +543,8 @@
     weights = take(4)
     qkv_w, out_w, up_w, down_w = weights
     landings = [take(CHIP_AXES + 1) for _ in range(CHUNKS)]
-    normed, qkv, mixed, mixed_rest, grad_mixed, branch, lse, staging = take(8)
+    normed, qkv, mixed, mixed_rest, grad_mixed, lse, staging, down_g, out_g = take(9)
+    branch = mixed_rest
     my_rows, pair_rows, biases, small_values, small_landing, sum_values, sum_landing = take(7)
     (
         pair_send, pair_recv, small_send, small_recv, sum_send, sum_recv,
@@ -653,16 +664,20 @@
 
     lax.fori_loop(0, pairs, forward, 0)
     save.wait()
+    pltpu.make_async_copy(mixed_rest, rest_away, row_sems.at[3]).start()
 
     sums = sum_values.at[0]
     sums[...] = jnp.zeros(sums.shape, f32)
-    reduces = [
-        ReduceChunk(
-            place, REDUCE_ORDERS[index], view, (slice(None),) * len(lead),
-            landings[index], reduce_send.at[index], reduce_recv.at[index],
-        )
-        for index, (view, lead, _) in enumerate(weight_chunks(weights))
-    ]
+    def reduce_chunks(qkv_g):
+        return [
+            ReduceChunk(
+                place, REDUCE_ORDERS[index], view, (slice(None),) * len(lead),
+                landings[index], reduce_send.at[index], reduce_recv.at[index],
+            )
+            for index, (view, lead, _) in enumerate(weight_chunks((qkv_g, out_g, up_w, down_g)))
+        ]
+
+    reduces = reduce_chunks(qkv_w)
 
     def emit_rows(target, block, sem, values):
         rows = pl.ds(aligned(block * ROWS, ROWS), ROWS)
@@ -677,7 +692,14 @@
     def emit_last(target, sem):
         pltpu.make_async_copy(staging, target.at[pl.ds(0, ROWS), :], sem).wait()
 
-    def feed_forward(grad_pre, whole_cotangent, normed_t, out_total, grad_total):
+    def reduce_steps(where):
+        for chunk, stage in REDUCE_STEPS[where]:
+            reduces[chunk].absorb(stage)
+
+    def absorb(chunk, stage):
+        reduces[chunk].absorb(stage)
+
+    def feed_forward(grad_pre, normed_t, grad_total):
         def normed_body(block, carry):
             rows = pl.ds(aligned(block * ROWS, ROWS), ROWS)
             feed_normed_rows(rows, resid, mixed, small, biases, out_w, grad_mixed, normed_t)
@@ -696,34 +718,46 @@
             return carry
 
         lax.fori_loop(0, len(after_up), there, 0)
+
+        def grad_down(part, carry):
+            columns = pl.ds(aligned(part * FF_BLOCK, FF_BLOCK), FF_BLOCK)
+            down_g[lax.div(part, 2), lax.rem(part, 2)] = (
+                dot(activated[:, columns], cotangent[...], TN)
+                .astype(bf16)
+                .reshape(down_g.shape[2:])
+            )
+            after(
+                4, part, lambda which: GATHER_STEPS["GRAD_DOWN"][which],
+                lambda chunk, stage: gathers[chunk].step(stage),
+            )
+            return carry
+
+        lax.fori_loop(0, up_w.shape[-1] // FF_BLOCK, grad_down, 0)
+        reduces[DOWN_A].launch(0)
+        reduces[DOWN_B].launch(0)
+        keep = pltpu.make_async_copy(activated, activated_away, row_sems.at[0])
+        keep.start()
         gather_steps("BACK")
         for chunk in gathers:
             chunk.drain()
+        reduce_steps("STARTED")
+        pltpu.make_async_copy(mixed_rest, rest_away, row_sems.at[3]).wait()
+        keep.wait()
+        pltpu.make_async_copy(qkv_away, qkv, row_sems.at[4]).start()
 
         def back(block, carry):
             rows = pl.ds(aligned(block * ROWS, ROWS), ROWS)
             feed_backward_rows(
-                rows, block == 0, resid, cotangent, mixed, small, biases, weights, activated,
-                grad_pre, (branch, grad_mixed, whole_cotangent), (out_total, grad_total), sums,
-                partial(emit_rows, out_resid, block, row_sems.at[1]),
+                rows, block == 0, resid, cotangent, mixed, small, biases, weights,
+                grad_pre, branch, grad_mixed, grad_total, sums,
+            )
+            after(
+                blocks, block, lambda which: REDUCE_STEPS["BACK"][which],
+                lambda chunk, stage: reduces[chunk].absorb(stage),
             )
             return carry
 
         lax.fori_loop(0, blocks, back, 0)
-
-        def grad_down(part, carry):
-            columns = pl.ds(aligned(part * FF_BLOCK, FF_BLOCK), FF_BLOCK)
-            down_w[lax.div(part, 2), lax.rem(part, 2)] = (
-                dot(activated[:, columns], whole_cotangent[...], TN)
-                .astype(bf16)
-                .reshape(down_w.shape[2:])
-            )
-            return carry
-
-        lax.fori_loop(0, up_w.shape[-1] // FF_BLOCK, grad_down, 0)
-        reduces[DOWN_A].launch(0)
-        reduces[DOWN_B].launch(0)
-        pltpu.make_async_copy(qkv_away, qkv, row_sems.at[4]).start()
 
         def grad_up(part, carry):
             columns = pl.ds(aligned(part * FF_BLOCK, FF_BLOCK), FF_BLOCK)
@@ -744,38 +778,35 @@
 
         def grad_out(half, carry):
             columns = pl.ds(aligned(half * (D // 2), LANES), D // 2)
-            out_w[half] = (
-                dot(mixed[:, columns], branch[...], TN).astype(bf16).reshape(out_w.shape[1:])
+            out_g[half] = (
+                dot(mixed[:, columns], branch[...], TN).astype(bf16).reshape(out_g.shape[1:])
             )
             return carry
 
         lax.fori_loop(0, 2, grad_out, 0)
         reduces[OUT].launch(0)
-        emit_last(out_resid, row_sems.at[1])
 
     pl.run_scoped(
         feed_forward,
         pltpu.VMEM((count, up_w.shape[-1]), bf16),
-        pltpu.VMEM((count, D), bf16),
         pltpu.VMEM((D, count), bf16),
         pltpu.VMEM((ROWS, D), f32),
-        pltpu.VMEM((ROWS, D), f32),
     )
     pltpu.make_async_copy(qkv_away, qkv, row_sems.at[4]).wait()
 
-    def reduce_steps(where):
-        for chunk, stage in REDUCE_STEPS[where]:
-            reduces[chunk].absorb(stage)
-
-    def attention_backward(grad_normed, lse_t, delta_t, grad_query, normed_t):
+    def attention_backward(qkv_g, row_total, lse_t, delta_t, grad_query, normed_t):
+        reduces[:] = reduce_chunks(qkv_g)
+
         def turn(block, carry):
             rows = pl.ds(aligned(block * ROWS, ROWS), ROWS)
             normed_t[:, rows] = jnp.transpose(normed[rows, :])
-            grad_normed[rows, :] = jnp.zeros((ROWS, D), f32)
             return carry
 
         lax.fori_loop(0, blocks, turn, 0)
-        backward_rows(mixed, mixed_rest, grad_mixed, lse, lse_t, delta_t)
+        back_again = pltpu.make_async_copy(rest_away, normed, row_sems.at[3])
+        back_again.start()
+        back_again.wait()
+        backward_rows(mixed, normed, grad_mixed, lse, lse_t, delta_t)
         reduce_steps("PREPARED")
         ticks = REDUCE_STEPS["BACKWARD"]
 
@@ -785,20 +816,9 @@
             def grad_columns(part):
                 return pl.ds(aligned(part * D + group * GROUP, GROUP), GROUP)
 
-            def of_rows(block, carry):
-                rows = pl.ds(aligned(block * ROWS, ROWS), ROWS)
-                total = grad_normed[rows, :]
-                for part in range(3):
-                    weight = qkv_w[part, :, :, :, :, :, columns].reshape(D, GROUP)
-                    total = total + dot(qkv[rows, grad_columns(part)], weight, NT)
-                grad_normed[rows, :] = total
-                return carry
-
-            lax.fori_loop(0, blocks, of_rows, 0)
-
             def of_weight(part, carry):
                 grads = qkv[:, grad_columns(part)]
-                qkv_w[part, :, :, :, :, :, columns] = (
+                qkv_g[part, :, :, :, :, :, columns] = (
                     dot(normed_t[...], grads)
                     .astype(bf16)
                     .reshape((2,) * CHIP_AXES + (BLOCK, GROUP))
@@ -818,7 +838,7 @@
                         pairs, pair, lambda which: ticks[which * TICKS + turn],
                         lambda chunk, stage: reduces[chunk].absorb(stage),
                     )
-            qkv[:, pair_columns(pair)[0]] = grad_query[...].astype(bf16)
+            qkv[:, pair_columns(pair)[0]] = jnp.transpose(grad_query[...]).astype(bf16)
 
             @pl.when(lax.rem(pair, per_group) == per_group - 1)
             def _():
@@ -841,11 +861,19 @@
 
         lax.fori_loop(0, pairs, backward, 0)
 
-        def body(block, carry):
+        def resid_rows(block, carry):
             rows = pl.ds(aligned(block * ROWS, ROWS), ROWS)
+            row_total[...] = jnp.zeros(row_total.shape, f32)
+
+            def add(part, carry):
+                grads = qkv[rows, pl.ds(aligned(part * D, D), D)]
+                row_total[...] = row_total[...] + dot(grads, qkv_w[part].reshape(D, D), NT)
+                return carry
+
+            lax.fori_loop(0, 3, add, 0)
             full = complete(widen(resid[rows, :].astype(f32)))
             gain_terms, grad_input = norm_backward(
-                grad_normed[rows, :], full, inverse_size(full), small[pl.ds(0, 1), :]
+                row_total[...], full, inverse_size(full), small[pl.ds(0, 1), :]
             )
             emit_rows(
                 grad_resid, block, row_sems.at[2],
@@ -853,78 +881,90 @@
             )
             total = column_sum(gain_terms)
             sums[pl.ds(0, 1), :] = jnp.where(block == 0, total, sums[pl.ds(0, 1), :] + total)
+            after(blocks, block, lambda which: REDUCE_STEPS["RESID"][which], absorb)
             return carry
 
-        lax.fori_loop(0, count // ROWS, body, 0)
+        lax.fori_loop(0, blocks, resid_rows, 0)
+        reload = pltpu.make_async_copy(activated_away, activated, row_sems.at[0])
+        reload.start()
+        sum_all = SmallSum(place, sum_values, sum_landing, sum_send, sum_recv)
+        sum_all.copy(0).start()
+        reload.wait()
+        emit_last(grad_resid, row_sems.at[2])
+
+        def out_rows(block, carry):
+            rows = pl.ds(aligned(block * ROWS, ROWS), ROWS)
+            values = feed_out_rows(rows, resid, mixed, biases, out_w, down_w, activated, row_total)
+            emit_rows(out_resid, block, row_sems.at[1], values)
+            after(blocks, block, lambda which: REDUCE_STEPS["OUT"][which], absorb)
+            for which in range(blocks):
+                @pl.when(block == which)
+                def _():
+                    sum_all.step(which)
+
+            return carry
+
+        lax.fori_loop(0, blocks, out_rows, 0)
+        for axis in range(blocks, CORE + 1):
+            sum_all.step(axis)
+        reduce_steps("REST")
+        small_out[...] = sum_values[5]
+
+        for chunk, start in ((DOWN_A, 0), (DOWN_B, D // 2)):
+            down_out[:, pl.ds(start, D // 2)] = reduces[chunk].total()
+        their_rows = pl.ds(aligned((1 - core) * shard_rows, 8), shard_rows)
+        kept_rows = pl.ds(aligned(core * shard_rows, 8), shard_rows)
+        copies = []
+
+        def deliver(slot, part_of, target):
+            away = send(
+                place, CORE, part_of(their_rows), target, final_send.at[slot], final_recv.at[slot]
+            )
+            away.start()
+            home = pltpu.make_async_copy(part_of(kept_rows), target, final_own.at[slot])
+            home.start()
+            copies.extend((away, home))
+
+        finals = pair_rows
+        half = up_w.shape[-1] // 4
+        finals[:, pl.ds(0, half)] = reduces[UP_A].total()
+        finals[:, pl.ds(half, half)] = reduces[UP_B].total()
+        deliver(
+            0, lambda rows: finals.at[rows, pl.ds(0, 2 * half)],
+            up_out.at[:, pl.ds(aligned(core * 2 * half, LANES), 2 * half)],
+        )
+        first = 2 * half
+        finals[:, pl.ds(first, D // 2)] = reduces[OUT].total()
+        deliver(
+            1, lambda rows: finals.at[rows, pl.ds(2 * half, D // 2)],
+            out_out.at[:, pl.ds(aligned(core * (D // 2), LANES), D // 2)],
+        )
+        first += D // 2
+        for group in range(GROUPS):
+            total = reduces[group].total()
+            for part in range(3):
+                here = pl.ds(first, LANES)
+                finals[:, here] = total[part]
+                deliver(
+                    2 + group * 3 + part, lambda rows, here=here: finals.at[rows, here],
+                    qkv_out.at[:, pl.ds(aligned(part * D + group * GROUP + core * LANES, LANES), LANES)],
+                )
+                first += LANES
+        for copy in copies:
+            copy.wait()
+        for chunk in reduces:
+            chunk.drain()
+        emit_last(out_resid, row_sems.at[1])
 
     pl.run_scoped(
         attention_backward,
-        pltpu.VMEM((count, D), f32),
+        pltpu.VMEM(qkv_w.shape, bf16),
+        pltpu.VMEM((ROWS, D), f32),
         pltpu.VMEM((16, count), f32),
         pltpu.VMEM((16, count), f32),
-        pltpu.VMEM((count, LANES), f32),
+        pltpu.VMEM((LANES, count), f32),
         pltpu.VMEM((D, count), bf16),
     )
-    sum_all = SmallSum(place, sum_values, sum_landing, sum_send, sum_recv)
-    sum_all.copy(0).start()
-    reduce_steps("NORM")
-    rest = REDUCE_STEPS["REST"]
-    axis = 0
-    for number, (chunk, stage) in enumerate(rest):
-        reduces[chunk].absorb(stage)
-        if axis < CORE:
-            sum_all.step(axis)
-            axis += 1
-    while axis <= CORE:
-        sum_all.step(axis)
-        axis += 1
-    small_out[...] = sum_values[5]
-
-    for chunk, start in ((DOWN_A, 0), (DOWN_B, D // 2)):
-        down_out[:, pl.ds(start, D // 2)] = reduces[chunk].total()
-    their_rows = pl.ds(aligned((1 - core) * shard_rows, 8), shard_rows)
-    kept_rows = pl.ds(aligned(core * shard_rows, 8), shard_rows)
-    copies = []
-
-    def deliver(slot, part_of, target):
-        away = send(
-            place, CORE, part_of(their_rows), target, final_send.at[slot], final_recv.at[slot]
-        )
-        away.start()
-        home = pltpu.make_async_copy(part_of(kept_rows), target, final_own.at[slot])
-        home.start()
-        copies.extend((away, home))
-
-    finals = pair_rows
-    half = up_w.shape[-1] // 4
-    finals[:, pl.ds(0, half)] = reduces[UP_A].total()
-    finals[:, pl.ds(half, half)] = reduces[UP_B].total()
-    deliver(
-        0, lambda rows: finals.at[rows, pl.ds(0, 2 * half)],
-        up_out.at[:, pl.ds(aligned(core * 2 * half, LANES), 2 * half)],
-    )
-    first = 2 * half
-    finals[:, pl.ds(first, D // 2)] = reduces[OUT].total()
-    deliver(
-        1, lambda rows: finals.at[rows, pl.ds(2 * half, D // 2)],
-        out_out.at[:, pl.ds(aligned(core * (D // 2), LANES), D // 2)],
-    )
-    first += D // 2
-    for group in range(GROUPS):
-        total = reduces[group].total()
-        for part in range(3):
-            here = pl.ds(first, LANES)
-            finals[:, here] = total[part]
-            deliver(
-                2 + group * 3 + part, lambda rows, here=here: finals.at[rows, here],
-                qkv_out.at[:, pl.ds(aligned(part * D + group * GROUP + core * LANES, LANES), LANES)],
-            )
-            first += LANES
-    for copy in copies:
-        copy.wait()
-    for chunk in reduces:
-        chunk.drain()
-    emit_last(grad_resid, row_sems.at[2])
 
 
 def layer_by_kernel(resid, cotangent, qkv_in, out_in, up_in, down_in, small_in, biases, lengths):
@@ -955,9 +995,10 @@
             pltpu.VMEM((count, D), bf16),
             pltpu.VMEM((count, D), bf16),
             pltpu.VMEM((count, D), bf16),
-            pltpu.VMEM((count, D), bf16),
             pltpu.VMEM((count, LANES), f32),
             pltpu.VMEM((ROWS, D), bf16),
+            pltpu.VMEM(weight_shapes[3], bf16),
+            pltpu.VMEM(weight_shapes[1], bf16),
             pltpu.VMEM((BLOCK, (3 * D + D + ff) // 2), f32),
             pltpu.VMEM((BLOCK, (3 * D + D + ff) // 2), f32),
             pltpu.VMEM((2, D), f32),
@@ -995,9 +1036,11 @@
             jax.ShapeDtypeStruct((down_in.shape[0], D), f32),
             jax.ShapeDtypeStruct((sum_rows, D), f32),
             jax.ShapeDtypeStruct((count, 3 * D), bf16),
+            jax.ShapeDtypeStruct((count, D), bf16),
+            jax.ShapeDtypeStruct((count, ff), bf16),
         ],
         in_specs=[in_vmem] * 8 + [pl.BlockSpec(memory_space=pltpu.SMEM)],
-        out_specs=[in_hbm] * 2 + [in_vmem] * 5 + [in_hbm],
+        out_specs=[in_hbm] * 2 + [in_vmem] * 5 + [in_hbm] * 3,
         scratch_shapes=scratch,
         compiler_params=pltpu.CompilerParams(
             collective_id=1, has_side_effects=True, vmem_limit_bytes=VMEM_BYTES
@@ -1021,8 +1064,8 @@
     width = out_weight.shape[1]
     small = jnp.concatenate([gain_attn, gain_mlp, qv_bias, up_bias]).astype(f32)
     biases = jnp.stack([out_bias, down_bias]).astype(f32)
-    out_resid, grad_resid, qkv, out, up, down, sums, _ = layer_by_kernel(
-        resid, cotangent, qkv_weight, out_weight, up_weight, down_weight,
+    out_resid, grad_resid, qkv, out, up, down, sums, _, _, _ = layer_by_kernel(
+        resid, jnp.pad(cotangent, ((0, 0), (0, D - width))), qkv_weight, out_weight, up_weight, down_weight,
         small.reshape(1, -1), biases, seq_lengths,
     )
     sums = sums.reshape(-1)

time: 217 us -> 210 us (0.968)
  Pallas kernels: 203 us -> 195 us
    pallas_call x1, Pallas kernels: 203 us -> 195 us  [layer_by_kernel(): pl.pallas_call(layer_kernel, out_shape=[jax.ShapeDtypeStruct((count, D),...]
    pad x0 -> x1, local copies, waits for them, and re-layouts: none -> 2.74 us  [on_device_by_kernel(): jnp.pad(cotangent, ((0, 0), (0, D - width)))]
    unnamed x16 -> x28, local copies, waits for them, and re-layouts: 6.68 us -> 6.7 us
where the time goes in v3:
time: 210 us; the launch traced here: 209 us
  Pallas kernels  195 us (93%)
  local copies, waits for them, and re-layouts  12.6 us (6%)
    pallas_call x1, Pallas kernels, layer_by_kernel(): pl.pallas_call(layer_kernel, out_shape=[jax.ShapeDtypeStruct((count, D),...  195 us
    unnamed x28, local copies, waits for them, and re-layouts  6.7 us

profile of v3, /device:TPU:0, one launch (start us, length us, event | category | flops | bytes accessed | tf_op | source)
XLA Modules:
  0.0 209.2 jit_solution(9398464676707863032)
XLA Ops:
  0.6 0.0 copy-start.7
  0.7 0.0 copy-start.8
  0.7 0.0 copy-start.9
  0.7 0.0 copy-start.10
  0.7 0.0 copy-start.5
  0.7 0.0 copy-start.6
  0.7 2.7 %pad.4.cotangent = bf16[1024,768]{1,0:T(8,128)(2,1)} pad(bf16[1024,767]{1,0:T(8,128)(2,1)} %param.24, bf16[]{:T(256)} %constant.7.clone.1), padding=0_0x0_1 | pad | bytes 3143682 | tf_op jit(solution)/shard_map/jit(_pad)/pad | solution.py:1068
  3.4 0.0 copy-done.7
  3.4 0.0 copy-done.8
  3.5 0.0 copy-done.9
  3.5 0.0 copy-done.10
  3.5 0.6 maximum_convert_fusion.1.small_in
  4.1 0.0 copy-done.5
  4.1 0.0 copy-done.6
  4.1 0.6 maximum_convert_fusion.biases_in
  4.7 194.6 %layer.1 = (bf16[1024,768]{1,0:T(8,128)(2,1)}, bf16[1024,768]{1,0:T(8,128)(2,1)}, f32[24,2304]{1,0:T(8,128)}, f32[24,768]{1,0:T(8,128)}, f32[24,3072]{1,0:T(8,12...) custom-call(bf16[1024,767]{1,0:T(8,128)(2,1)} %resid.1, ...), custom_call_target="tpu_custom_call" | custom-call | tf_op jit(solution)/shard_map/layer/pallas_call | solution.py:1028
  199.4 0.8 reshape.83
  200.2 0.6 fusion.1
  200.8 0.6 dynamic_slice.13
  201.4 0.6 fusion
  202.0 0.6 dynamic_slice.15
  202.5 0.0 copy-start
  202.5 2.8 %copy.31 = bf16[1024,767]{1,0:T(8,128)(2,1)} copy(bf16[1024,767]{1,0:T(8,128)(2,1)} %bitcast.9) | data formatting | bytes 3141632
  205.3 0.0 copy-done
  205.3 0.0 copy-start.3
  205.3 0.0 copy-start.4
  205.3 0.0 copy-start.2
  205.3 0.0 copy-start.1
  205.3 1.1 copy.32
  206.5 0.0 copy-done.3
  206.5 0.7 copy.33
  207.2 0.0 copy-done.4
  207.2 0.6 copy.34
  207.8 0.0 copy-done.2
  207.8 0.7 copy.35
  208.5 0.0 copy-done.1
  208.5 0.7 copy.36
  (2 shorter events, 0.0 us)
Async XLA Ops:
  0.6 2.8 %copy-start.7 = (bf16[96]{0:T(256)(128)(2,1)S(1)}, bf16[96]{0:T(256)(128)(2,1)}, u32[]{:S(2)}) copy-start(bf16[96]{0:T(256)(128)(2,1)} %param.21) | copy-start | bytes 580
  0.7 2.8 %copy-start.8 = (bf16[48]{0:T(256)(128)(2,1)S(1)}, bf16[48]{0:T(256)(128)(2,1)}, u32[]{:S(2)}) copy-start(bf16[48]{0:T(256)(128)(2,1)} %param.16) | copy-start | bytes 292
  0.7 2.8 %copy-start.9 = (bf16[24]{0:T(256)(128)(2,1)S(1)}, bf16[24]{0:T(256)(128)(2,1)}, u32[]{:S(2)}) copy-start(bf16[24]{0:T(256)(128)(2,1)} %param.19) | copy-start | bytes 148
  0.7 2.8 %copy-start.10 = (bf16[24]{0:T(256)(128)(2,1)S(1)}, bf16[24]{0:T(256)(128)(2,1)}, u32[]{:S(2)}) copy-start(bf16[24]{0:T(256)(128)(2,1)} %param.14) | copy-start | bytes 148
  0.7 3.4 %copy-start.5 = (bf16[767]{0:T(1024)(128)(2,1)S(1)}, bf16[767]{0:T(1024)(128)(2,1)}, u32[]{:S(2)}) copy-start(bf16[767]{0:T(1024)(128)(2,1)} %param.23) | copy-start | bytes 4606
  0.7 3.4 %copy-start.6 = (bf16[767]{0:T(1024)(128)(2,1)S(1)}, bf16[767]{0:T(1024)(128)(2,1)}, u32[]{:S(2)}) copy-start(bf16[767]{0:T(1024)(128)(2,1)} %param.18) | copy-start | bytes 4606
  202.5 2.8 %copy-start = (bf16[1024,768]{1,0:T(8,128)(2,1)S(1)}, bf16[1024,768]{1,0:T(8,128)(2,1)}, u32[]{:S(2)}) copy-start(bf16[1024,768]{1,0:T(8,128)(2,1)} %get-tuple-element.20) | copy-start | bytes 4718596
  205.3 1.2 copy-start.3
  205.3 1.9 copy-start.4
  205.3 2.5 %copy-start.2 = (f32[24,3072]{1,0:T(8,128)S(1)}, f32[24,3072]{1,0:T(8,128)}, u32[]{:S(2)}) copy-start(f32[24,3072]{1,0:T(8,128)} %get-tuple-element.50) | copy-start | bytes 884740
  205.3 3.2 %copy-start.1 = (f32[96,768]{1,0:T(8,128)S(1)}, f32[96,768]{1,0:T(8,128)}, u32[]{:S(2)}) copy-start(f32[96,768]{1,0:T(8,128)} %get-tuple-element.25) | copy-start | bytes 884740

commit v4 on v3

--- a/solution.py
+++ b/solution.py
@@ -264,9 +264,9 @@
     "PREPARED": [(UP_A, 0), (UP_B, 0), (OUT, 0), (DOWN_A, 2)],
     "BACKWARD": [[], [(DOWN_B, 2)], [(DOWN_A, 3)], [], [(DOWN_B, 3)], [(Q0, 0)], [(UP_B, 1)], [(UP_A, 1)], [], [(Q0, 1), (Q1, 0), (OUT, 1)], [], []],
     "FINISHED": [[], [], [(UP_A, 2), (UP_B, 2)]],
-    "RESID": [[], [(Q0, 2), (Q2, 0), (OUT, 2)], [(UP_A, 3)], []],
-    "OUT": [[(Q1, 1), (UP_B, 3)], [(Q0, 3)], [(Q2, 1), (OUT, 3)], []],
-    "REST": [(Q1, 2), (Q2, 2), (Q1, 3), (Q2, 3)],
+    "RESID": [[(Q2, 0)], [(Q0, 2), (OUT, 2)], [(UP_A, 3), (Q1, 1)], [(UP_B, 3)]],
+    "OUT": [[(Q0, 3), (Q2, 1)], [(OUT, 3)], [(Q1, 2)], [(Q2, 2)]],
+    "REST": [(Q1, 3), (Q2, 3)],
 }
 
 
@@ -549,8 +549,8 @@
     (
         pair_send, pair_recv, small_send, small_recv, sum_send, sum_recv,
         gather_send, gather_recv, reduce_send, reduce_recv,
-        final_send, final_recv, final_own, row_sems,
-    ) = take(14)
+        final_send, final_recv, final_own, row_sems, block_sems,
+    ) = take(15)
     activated = qkv
     qkv = activated.at[:, pl.ds(0, 3 * D)]
     count = resid.shape[0]
@@ -686,7 +686,7 @@
         def _():
             pltpu.make_async_copy(staging, target.at[rows, :], sem).wait()
 
-        staging[...] = values
+        staging[...] = values[:, : D - 1]
         pltpu.make_async_copy(staging, target.at[rows, :], sem).start()
 
     def emit_last(target, sem):
@@ -735,7 +735,7 @@
         lax.fori_loop(0, up_w.shape[-1] // FF_BLOCK, grad_down, 0)
         reduces[DOWN_A].launch(0)
         reduces[DOWN_B].launch(0)
-        keep = pltpu.make_async_copy(activated, activated_away, row_sems.at[0])
+        keep = pltpu.make_async_copy(qkv, activated_away, row_sems.at[0])
         keep.start()
         gather_steps("BACK")
         for chunk in gathers:
@@ -800,12 +800,17 @@
         def turn(block, carry):
             rows = pl.ds(aligned(block * ROWS, ROWS), ROWS)
             normed_t[:, rows] = jnp.transpose(normed[rows, :])
+            pltpu.make_async_copy(
+                rest_away.at[rows, :], normed.at[rows, :], block_sems.at[block]
+            ).start()
             return carry
 
         lax.fori_loop(0, blocks, turn, 0)
-        back_again = pltpu.make_async_copy(rest_away, normed, row_sems.at[3])
-        back_again.start()
-        back_again.wait()
+        for block in range(blocks):
+            rows = pl.ds(block * ROWS, ROWS)
+            pltpu.make_async_copy(
+                rest_away.at[rows, :], normed.at[rows, :], block_sems.at[block]
+            ).wait()
         backward_rows(mixed, normed, grad_mixed, lse, lse_t, delta_t)
         reduce_steps("PREPARED")
         ticks = REDUCE_STEPS["BACKWARD"]
@@ -861,6 +866,12 @@
 
         lax.fori_loop(0, pairs, backward, 0)
 
+        def reload(block):
+            rows = pl.ds(aligned(block * ROWS, ROWS), ROWS)
+            return pltpu.make_async_copy(
+                activated_away.at[rows, :], qkv.at[rows, :], block_sems.at[block]
+            )
+
         def resid_rows(block, carry):
             rows = pl.ds(aligned(block * ROWS, ROWS), ROWS)
             row_total[...] = jnp.zeros(row_total.shape, f32)
@@ -881,19 +892,18 @@
             )
             total = column_sum(gain_terms)
             sums[pl.ds(0, 1), :] = jnp.where(block == 0, total, sums[pl.ds(0, 1), :] + total)
+            reload(block).start()
             after(blocks, block, lambda which: REDUCE_STEPS["RESID"][which], absorb)
             return carry
 
         lax.fori_loop(0, blocks, resid_rows, 0)
-        reload = pltpu.make_async_copy(activated_away, activated, row_sems.at[0])
-        reload.start()
         sum_all = SmallSum(place, sum_values, sum_landing, sum_send, sum_recv)
         sum_all.copy(0).start()
-        reload.wait()
         emit_last(grad_resid, row_sems.at[2])
 
         def out_rows(block, carry):
             rows = pl.ds(aligned(block * ROWS, ROWS), ROWS)
+            reload(block).wait()
             values = feed_out_rows(rows, resid, mixed, biases, out_w, down_w, activated, row_total)
             emit_rows(out_resid, block, row_sems.at[1], values)
             after(blocks, block, lambda which: REDUCE_STEPS["OUT"][which], absorb)
@@ -907,7 +917,6 @@
         lax.fori_loop(0, blocks, out_rows, 0)
         for axis in range(blocks, CORE + 1):
             sum_all.step(axis)
-        reduce_steps("REST")
         small_out[...] = sum_values[5]
 
         for chunk, start in ((DOWN_A, 0), (DOWN_B, D // 2)):
@@ -940,8 +949,14 @@
             out_out.at[:, pl.ds(aligned(core * (D // 2), LANES), D // 2)],
         )
         first += D // 2
-        for group in range(GROUPS):
+        late = [chunk for chunk, _ in REDUCE_STEPS["REST"]]
+        groups = sorted(range(GROUPS), key=lambda group: group in late)
+        for group in groups:
+            if group in late:
+                reduce_steps("REST")
+                late = []
             total = reduces[group].total()
+            first = 2 * half + D // 2 + group * 3 * LANES
             for part in range(3):
                 here = pl.ds(first, LANES)
                 finals[:, here] = total[part]
@@ -996,7 +1011,7 @@
             pltpu.VMEM((count, D), bf16),
             pltpu.VMEM((count, D), bf16),
             pltpu.VMEM((count, LANES), f32),
-            pltpu.VMEM((ROWS, D), bf16),
+            pltpu.VMEM((ROWS, D - 1), bf16),
             pltpu.VMEM(weight_shapes[3], bf16),
             pltpu.VMEM(weight_shapes[1], bf16),
             pltpu.VMEM((BLOCK, (3 * D + D + ff) // 2), f32),
@@ -1020,6 +1035,7 @@
             dma((11,)),
             dma((11,)),
             dma((5,)),
+            dma((count // ROWS,)),
         ]
     )
     in_vmem = pl.BlockSpec(memory_space=pltpu.VMEM)
@@ -1028,8 +1044,8 @@
     return pl.pallas_call(
         layer_kernel,
         out_shape=[
-            jax.ShapeDtypeStruct((count, D), bf16),
-            jax.ShapeDtypeStruct((count, D), bf16),
+            jax.ShapeDtypeStruct((count, D - 1), bf16),
+            jax.ShapeDtypeStruct((count, D - 1), bf16),
             jax.ShapeDtypeStruct((shard_rows, 3 * D), f32),
             jax.ShapeDtypeStruct((shard_rows, D), f32),
             jax.ShapeDtypeStruct((shard_rows, ff), f32),
@@ -1037,7 +1053,7 @@
             jax.ShapeDtypeStruct((sum_rows, D), f32),
             jax.ShapeDtypeStruct((count, 3 * D), bf16),
             jax.ShapeDtypeStruct((count, D), bf16),
-            jax.ShapeDtypeStruct((count, ff), bf16),
+            jax.ShapeDtypeStruct((count, 3 * D), bf16),
         ],
         in_specs=[in_vmem] * 8 + [pl.BlockSpec(memory_space=pltpu.SMEM)],
         out_specs=[in_hbm] * 2 + [in_vmem] * 5 + [in_hbm] * 3,
@@ -1077,8 +1093,8 @@
     ff = up_weight.shape[1]
     last = 4 * D + ff
     return (
-        out_resid[:, :width],
-        grad_resid[:, :width],
+        out_resid,
+        grad_resid,
         shard(0, D),
         qkv,
         shard(2 * D, 2 * D),

time: 210 us -> 209 us (level)
  no operation moved by 1% of the time
where the time goes in v4:
time: 209 us
  Pallas kernels  194 us (93%)
  local copies, waits for them, and re-layouts  12.6 us (6%)
    pallas_call x1, Pallas kernels, layer_by_kernel(): pl.pallas_call(layer_kernel, out_shape=[jax.ShapeDtypeStruct((count, D -...  194 us
    unnamed x28, local copies, waits for them, and re-layouts  6.7 us

profile of v4, /device:TPU:0, one launch (start us, length us, event | category | flops | bytes accessed | tf_op | source)
XLA Modules:
  0.0 208.6 jit_solution(14062340609201093494)
XLA Ops:
  0.6 0.0 copy-start.7
  0.7 0.0 copy-start.8
  0.7 0.0 copy-start.9
  0.7 0.0 copy-start.10
  0.7 0.0 copy-start.5
  0.7 0.0 copy-start.6
  0.7 2.7 %pad.4.cotangent = bf16[1024,768]{1,0:T(8,128)(2,1)} pad(bf16[1024,767]{1,0:T(8,128)(2,1)} %param.24, bf16[]{:T(256)} %constant.7.clone.1), padding=0_0x0_1 | pad | bytes 3143682 | tf_op jit(solution)/shard_map/jit(_pad)/pad | solution.py:1084
  3.4 0.0 copy-done.7
  3.4 0.0 copy-done.8
  3.5 0.0 copy-done.9
  3.5 0.0 copy-done.10
  3.5 0.6 maximum_convert_fusion.1.small_in
  4.1 0.0 copy-done.5
  4.1 0.0 copy-done.6
  4.1 0.6 maximum_convert_fusion.biases_in
  4.7 194.0 %layer.1 = (bf16[1024,767]{1,0:T(8,128)(2,1)}, bf16[1024,767]{1,0:T(8,128)(2,1)}, f32[24,2304]{1,0:T(8,128)}, f32[24,768]{1,0:T(8,128)}, f32[24,3072]{1,0:T(8,12...) custom-call(bf16[1024,767]{1,0:T(8,128)(2,1)} %resid.1, ...), custom_call_target="tpu_custom_call" | custom-call | tf_op jit(solution)/shard_map/layer/pallas_call | solution.py:1044
  198.8 0.8 reshape.83
  199.6 0.6 fusion.1
  200.2 0.6 dynamic_slice.13
  200.8 0.6 fusion
  201.4 0.6 dynamic_slice.15
  201.9 0.0 copy-start
  201.9 2.8 %copy.31 = bf16[1024,767]{1,0:T(8,128)(2,1)} copy(bf16[1024,767]{1,0:T(8,128)(2,1)} %get-tuple-element.42) | data formatting | bytes 3141632
  204.7 0.0 copy-done
  204.7 0.0 copy-start.3
  204.7 0.0 copy-start.4
  204.7 0.0 copy-start.2
  204.7 0.0 copy-start.1
  204.7 1.1 copy.32
  205.9 0.0 copy-done.3
  205.9 0.7 copy.33
  206.6 0.0 copy-done.4
  206.6 0.6 copy.34
  207.2 0.0 copy-done.2
  207.2 0.7 copy.35
  207.9 0.0 copy-done.1
  207.9 0.7 copy.36
  (2 shorter events, 0.0 us)
Async XLA Ops:
  0.6 2.8 %copy-start.7 = (bf16[96]{0:T(256)(128)(2,1)S(1)}, bf16[96]{0:T(256)(128)(2,1)}, u32[]{:S(2)}) copy-start(bf16[96]{0:T(256)(128)(2,1)} %param.21) | copy-start | bytes 580
  0.7 2.8 %copy-start.8 = (bf16[48]{0:T(256)(128)(2,1)S(1)}, bf16[48]{0:T(256)(128)(2,1)}, u32[]{:S(2)}) copy-start(bf16[48]{0:T(256)(128)(2,1)} %param.16) | copy-start | bytes 292
  0.7 2.8 %copy-start.9 = (bf16[24]{0:T(256)(128)(2,1)S(1)}, bf16[24]{0:T(256)(128)(2,1)}, u32[]{:S(2)}) copy-start(bf16[24]{0:T(256)(128)(2,1)} %param.19) | copy-start | bytes 148
  0.7 2.8 %copy-start.10 = (bf16[24]{0:T(256)(128)(2,1)S(1)}, bf16[24]{0:T(256)(128)(2,1)}, u32[]{:S(2)}) copy-start(bf16[24]{0:T(256)(128)(2,1)} %param.14) | copy-start | bytes 148
  0.7 3.4 %copy-start.5 = (bf16[767]{0:T(1024)(128)(2,1)S(1)}, bf16[767]{0:T(1024)(128)(2,1)}, u32[]{:S(2)}) copy-start(bf16[767]{0:T(1024)(128)(2,1)} %param.23) | copy-start | bytes 4606
  0.7 3.4 %copy-start.6 = (bf16[767]{0:T(1024)(128)(2,1)S(1)}, bf16[767]{0:T(1024)(128)(2,1)}, u32[]{:S(2)}) copy-start(bf16[767]{0:T(1024)(128)(2,1)} %param.18) | copy-start | bytes 4606
  201.9 2.8 %copy-start = (bf16[1024,767]{1,0:T(8,128)(2,1)S(1)}, bf16[1024,767]{1,0:T(8,128)(2,1)}, u32[]{:S(2)}) copy-start(bf16[1024,767]{1,0:T(8,128)(2,1)} %get-tuple-element.43) | copy-start | bytes 4712452
  204.7 1.2 copy-start.3
  204.7 1.9 copy-start.4
  204.7 2.5 %copy-start.2 = (f32[24,3072]{1,0:T(8,128)S(1)}, f32[24,3072]{1,0:T(8,128)}, u32[]{:S(2)}) copy-start(f32[24,3072]{1,0:T(8,128)} %get-tuple-element.50) | copy-start | bytes 884740
  204.7 3.2 %copy-start.1 = (f32[96,768]{1,0:T(8,128)S(1)}, f32[96,768]{1,0:T(8,128)}, u32[]{:S(2)}) copy-start(f32[96,768]{1,0:T(8,128)} %get-tuple-element.25) | copy-start | bytes 884740
